TPU v7x, 128 devices: a whole 4x4x4 slice. The times are simulated.
128 devices in a mesh: layer: 8 (over x, z_hi), seq: 16 (over z_lo, y, core).
Axes of the slice: x: 4, y: 4, z: 4 (z_hi: 2, z_lo: 2; z = z_hi * 2 + z_lo), core: 2. Of those that a mesh axis runs over, the one named last changes fastest.
Arguments:
- panels: bfloat16 [8, 2560, 2048], P('layer', 'seq'), may hold values from -6 to 6
- feed: bfloat16 [2, 2560, 2048], P(None, 'seq'), may hold values from -6 to 6
- ssm_state: float32 [8, 16, 64, 64, 128], P('layer', 'seq'), may hold values from -6 to 6
- conv_state: bfloat16 [8, 16, 3, 5120], P('layer', 'seq'), may hold values from -6 to 6
- w_in: bfloat16 [8, 2048, 9280], P('layer', 'seq'), may hold values from -0.125 to 0.125
- w_out: bfloat16 [8, 4096, 2048], P('layer'), may hold values from -0.09375 to 0.09375
- norm_gain: float32 [8, 2048], P('layer'), may hold values from 0.25 to 1.75
- conv_weight: float32 [8, 4, 5120], P('layer'), may hold values from -3 to 3
- conv_bias: float32 [8, 5120], P('layer'), may hold values from -3 to 3
- dt_bias: float32 [8, 64], P('layer'), may hold values from -3 to 0
- decay_rate: float32 [8, 64], P('layer'), may hold values from 0.01 to 2
- skip_gain: float32 [8, 64], P('layer'), may hold values from 0.5 to 2
- out_gain: float32 [8, 4096], P('layer'), may hold values from 0.25 to 1.75
Outputs:
- panels_out: bfloat16 [8, 2560, 2048], P('layer', 'seq')
- states_out: float32 [8, 16, 64, 64, 128], P('layer', 'seq')
All inputs are finite; a program needn't handle non-finite values.
Results may differ from a plain program's by a relative error of at most 0.015.
Values may be sent and summed in bfloat16 or wider, within the bound.
A program may use at most 192 MiB of HBM per device.

v0:
```python
import jax
import jax.numpy as jnp
from jax import lax
from jax.sharding import PartitionSpec as P

HEADS = 64
HEAD_DIM = 64
STATE = 128
GROUPS = 4
KERNEL = 4
TURNS = 3
INNER = 4096
CONV_CH = 5120


EPS = 1e-05


def from_behind(block, axis, distance):
    devices = range(lax.axis_size(axis))
    route = [(i - distance, i) for i in devices if i - distance in devices]
    return lax.ppermute(block, axis, route)


def rms_scale(values, gain):
    return values * lax.rsqrt(jnp.mean(values * values, axis=-1, keepdims=True) + EPS) * gain


def mixer_core(
    projected, state_now, tail_now, conv_weight, conv_bias, dt_bias, decay_rate, skip_gain, out_gain
):
    row_count = projected.shape[0]
    per_group = HEADS // GROUPS
    highest = lax.Precision.HIGHEST
    gate_branch = projected[:, :INNER]
    conv_input = projected[:, INNER : INNER + CONV_CH].astype(jnp.bfloat16)
    step_logit = projected[:, INNER + CONV_CH :]
    window = jnp.concatenate([tail_now, conv_input], axis=0)
    conv_sum = jnp.zeros((row_count, CONV_CH), jnp.float32)
    for offset in range(KERNEL):
        conv_sum = (
            conv_sum + window[offset : offset + row_count].astype(jnp.float32) * conv_weight[offset]
        )
    activated = jax.nn.silu(conv_sum + conv_bias)
    ssm_input = (
        activated[:, :INNER].astype(jnp.bfloat16).reshape(row_count, GROUPS, per_group, HEAD_DIM)
    )
    write_map = (
        activated[:, INNER : INNER + GROUPS * STATE]
        .astype(jnp.bfloat16)
        .reshape(row_count, GROUPS, STATE)
    )
    read_map = (
        activated[:, INNER + GROUPS * STATE :]
        .astype(jnp.bfloat16)
        .reshape(row_count, GROUPS, STATE)
    )
    step_size = jax.nn.softplus(step_logit + dt_bias)
    log_decay = jnp.cumsum(-decay_rate * step_size, axis=0)
    head_decay = log_decay.T
    causal = jnp.arange(row_count)[:, None] >= jnp.arange(row_count)[None, :]
    decay_gap = head_decay[:, :, None] - head_decay[:, None, :]
    decay_mask = jnp.where(causal, jnp.exp(jnp.where(causal, decay_gap, 0.0)), 0.0)
    scores = jnp.einsum("tgn,sgn->gts", read_map, write_map, preferred_element_type=jnp.float32)
    weights = (
        scores[:, None]
        * decay_mask.reshape(GROUPS, per_group, row_count, row_count)
        * step_size.T.reshape(GROUPS, per_group, 1, row_count)
    ).astype(jnp.bfloat16)
    local_out = jnp.einsum(
        "ghts,sghp->tghp", weights, ssm_input, preferred_element_type=jnp.float32
    )
    read_wide = read_map.astype(jnp.float32)
    input_wide = ssm_input.astype(jnp.float32)
    state_view = state_now.reshape(GROUPS, per_group, HEAD_DIM, STATE)
    carried = jnp.einsum("tgn,ghpn->tghp", read_wide, state_view, precision=highest)
    carried = carried * jnp.exp(log_decay).reshape(row_count, GROUPS, per_group, 1)
    combined = local_out + carried + skip_gain.reshape(GROUPS, per_group, 1) * input_wide
    gated = combined.reshape(row_count, INNER) * jax.nn.silu(gate_branch)
    mixed_norm = rms_scale(gated, out_gain).astype(jnp.bfloat16)
    final_decay = log_decay[-1]
    end_weight = jnp.exp(final_decay[None, :] - log_decay) * step_size
    scaled_input = input_wide * end_weight.reshape(row_count, GROUPS, per_group, 1)
    new_state = jnp.exp(final_decay).reshape(GROUPS, per_group, 1, 1) * state_view
    new_state = new_state + jnp.einsum(
        "sghp,sgn->ghpn", scaled_input, write_map.astype(jnp.float32), precision=highest
    )
    return (
        mixed_norm,
        new_state.reshape(HEADS, HEAD_DIM, STATE),
        conv_input[row_count - (KERNEL - 1) :],
    )


def run_tile(panel_now, state_now, tail_now, in_full, out_full, small_params):
    norm_gain = small_params[0]
    normed = rms_scale(panel_now.astype(jnp.float32), norm_gain).astype(jnp.bfloat16)
    projected = jnp.dot(normed, in_full, preferred_element_type=jnp.float32)
    mixed_norm, new_state, new_tail = mixer_core(projected, state_now, tail_now, *small_params[1:])
    panel_out = (
        panel_now.astype(jnp.float32)
        + jnp.dot(mixed_norm, out_full, preferred_element_type=jnp.float32)
    ).astype(jnp.bfloat16)
    return (panel_out, new_state, new_tail)


def local(
    panels,
    feed,
    ssm_state,
    conv_state,
    w_in,
    w_out,
    norm_gain,
    conv_weight,
    conv_bias,
    dt_bias,
    decay_rate,
    skip_gain,
    out_gain,
):
    section_index = lax.axis_index("layer")
    panel_now = panels[0]
    state_now = ssm_state[0, 0]
    tail_now = conv_state[0, 0]
    small_params = (
        norm_gain[0],
        conv_weight[0],
        conv_bias[0],
        dt_bias[0],
        decay_rate[0],
        skip_gain[0],
        out_gain[0],
    )
    in_shard = w_in[0]
    out_full = w_out[0]
    in_full = lax.all_gather(in_shard, "seq", axis=0, tiled=True)
    first_turn = 0
    for step_index in range(TURNS):
        if step_index > 0:
            arrived = from_behind(panel_now, "layer", 1)
            panel_now = jnp.where(section_index == 0, feed[step_index - 1], arrived)
            state_now, tail_now = (
                from_behind(state_now.astype(jnp.bfloat16), "seq", 1).astype(state_now.dtype),
                from_behind(tail_now, "seq", 1),
            )
        panel_now, state_now, tail_now = run_tile(
            panel_now, state_now, tail_now, in_full, out_full, small_params
        )
    return (panel_now[None], state_now[None, None])


def solution(mesh):
    return jax.shard_map(
        local,
        mesh=mesh,
        in_specs=(
            P("layer", "seq", None),
            P(None, "seq", None),
            P("layer", "seq", None, None, None),
            P("layer", "seq", None, None),
            P("layer", "seq", None),
            P("layer", None, None),
            P("layer", None),
            P("layer", None, None),
            P("layer", None),
            P("layer", None),
            P("layer", None),
            P("layer", None),
            P("layer", None),
        ),
        out_specs=(P("layer", "seq", None), P("layer", "seq", None, None, None)),
        check_vma=False,
    )
```

profile of v0, /device:TPU:2, one launch (start us, length us, event | category | flops | bytes accessed | tf_op | source)
XLA Modules:
  0.0 468.1 jit_solution(16842732549143769541)
XLA Ops:
  7.2 0.7 all-gather.3.cloned.1.call-update
  8.4 1.3 reduce.21
  9.7 0.7 mul.448
  10.4 0.6 iota_compare_fusion
  11.0 1.3 fusion.78
  12.3 1.2 negate_bitcast_fusion
  13.5 1.2 fusion.129
  14.7 197.8 %all-gather.3.cloned.1.call-done = bf16[1,2048,9280]{1,2,0:T(8,128)(2,1)} async-done(((bf16[1,128,9280]{1,2,0:T(8,128)(2,1)}), bf16[1,2048,9280]{1,2,0:T(8,128)(2,1)}) %all-gather.3.cloned.1.call-update) | async-done | bytes 38010896 | tf_op jit(solution)/shard_map/all_gather | solution.py:137
  212.5 20.2 %fusion.130 = (bf16[160,9280]{1,0:T(8,128)(2,1)S(1)}, f32[160,9280]{1,0:T(8,128)}) fusion(bf16[1,2048,9280]{1,2,0:T(8,128)(2,1)} %all-gather.3.cloned.1.call-done, bf16[1,160,2048]{2,1,0:T(8,128)(2,1)} %param.13, f32[2048]{0:T(1024)} %bitcast.219, f32[160]{0:T(256)S(1)} %add_rsqrt_fusion.5), kind=kOutput, calls=%fused_computation.201 | convolution fusion | flops 6084536320 | bytes 47583872 | tf_op jit(solution)/shard_map/dot_general | solution.py:98
  233.6 2.4 multiply_convert_fusion.8
  236.0 0.9 fusion.128
  237.0 1.0 slice.225
  238.1 1.4 multiply_bitcast_fusion.2
  239.5 0.6 reduce-window.20
  240.6 1.6 reshape.209
  242.2 2.4 copy.165
  244.7 1.2 fusion.107
  246.0 2.9 fusion.121
  249.0 5.5 %fusion.33 = f32[160,4,16,64]{0,3,2,1:T(8,128)} fusion(bf16[160,4,16,64]{0,3,2,1:T(8,128)(2,1)S(1)} %bitcast.213, f32[4,160,16,64]{1,3,2,0:T(8,128)S(1)} %fusion.121, f32[4,16,160]{2,1,0:T(8,128)S(1)} %bitcast.245, f32[4,16,160]{2,1,0:T(8,128)S(1)} %bitcast.254, f32[4,160,160]{2,1,0:T(8,128)S(1)} %fusion.107, pred[160,160]{1,0:T(8,128)(4,1)S(1)} %copy-done.33, ...), kind=kOutput, calls=%fused_computation.42 | convolution fusion | flops 222822400 | bytes 7111936 | tf_op jit(solution)/shard_map/ghts,sghp->tghp/dot_general | solution.py:70
  254.5 3.9 copy.152
  258.4 2.7 multiply_reduce_fusion.2
  261.1 10.7 %fusion.57 = bf16[160,2048]{1,0:T(8,128)(2,1)} fusion(bf16[1,4096,2048]{2,1,0:T(8,128)(2,1)} %param.18, f32[4096]{0:T(1024)S(1)} %bitcast.259, f32[160]{0:T(256)S(1)} %add_rsqrt_fusion.4, bf16[1,160,2048]{2,1,0:T(8,128)(2,1)S(1)} %copy-done.8, f32[160,4096]{1,0:T(8,128)S(1)} %copy.152, f32[160,9280]{1,0:T(8,128)} %get-tuple-element.44), kind=kOutput, calls=%fused_computation.72 | convolution fusion | flops 2690580480 | bytes 23347840 | tf_op jit(solution)/shard_map/dot_general | solution.py:102
  271.8 5.2 %collective-permute-start = (bf16[160,2048]{1,0:T(8,128)(2,1)}, bf16[160,2048]{1,0:T(8,128)(2,1)S(1)}, u32[]{:S(2)}, u32[]{:S(2)}) collective-permute-start(bf16[160,2048]{1,0:T(8,128)(2,1)} %fusion.57), channel_id=1, source_target_pairs={{0,16},{16,32},{32,48},{48,64},{64,80},{80,96},{96,112},{1,17},{17... | collective-permute-start | bytes 1966088 | tf_op jit(solution)/shard_map/ppermute | solution.py:22
  277.0 0.9 slice.229
  277.9 1.9 collective-permute-start.1
  280.0 5.5 %add_convert_fusion.1 = bf16[4,16,64,128]{3,2,1,0:T(8,128)(2,1)} fusion(f32[4,16,64,128]{3,2,1,0:T(8,128)} %bitcast.210, bf16[160,4,16,64]{0,3,2,1:T(8,128)(2,1)} %bitcast.212, f32[160,4,16]{0,2,1:T(8,128)S(1)} %bitcast.239, f32[4,16]{1,0:T(4,128)S(1)} %exp.99, bf16[160,4,128,1]{2,1,0,3:T(4,128)(2,1)S(1)} %bitcast.224), kind=kOutput, calls=%fused_computation.84 | convolution fusion | flops 1009516544 | bytes 4661504 | tf_op jit(solution)/shard_map/sghp,sgn->ghpn/dot_general | solution.py:85
  285.4 4.3 collective-permute-start.2
  289.7 13.7 %collective-permute-done = bf16[160,2048]{1,0:T(8,128)(2,1)S(1)} collective-permute-done((bf16[160,2048]{1,0:T(8,128)(2,1)}, bf16[160,2048]{1,0:T(8,128)(2,1)S(1)}, u32[]{:S(2)}, u32[]{:S(2)}) %collective-permute-start) | collective-permute-done | bytes 655392 | tf_op jit(solution)/shard_map/ppermute | solution.py:22
  303.4 1.1 fusion.72
  304.5 20.5 %fusion.131 = (bf16[160,9280]{1,0:T(8,128)(2,1)S(1)}, f32[160,9280]{1,0:T(8,128)}) fusion(bf16[1,2048,9280]{1,2,0:T(8,128)(2,1)} %all-gather.3.cloned.1.call-done, bf16[160,2048]{1,0:T(8,128)(2,1)} %get-tuple-element.15, f32[160]{0:T(256)S(1)} %add_rsqrt_fusion.3, f32[2048]{0:T(1024)S(1)} %bitcast.220), kind=kOutput, calls=%fused_computation.202 | convolution fusion | flops 6084536320 | bytes 47583872 | tf_op jit(solution)/shard_map/dot_general | solution.py:98
  325.0 1.2 slice.238
  327.8 2.4 multiply_convert_fusion.7
  330.2 0.9 fusion.127
  331.1 0.7 exponential_multiply_fusion.1
  332.0 1.6 reshape.215
  333.6 1.8 copy.166
  335.5 1.6 fusion.102
  337.1 4.1 fusion.13
  341.3 4.2 fusion.35
  345.5 4.1 copy.157
  349.6 2.7 multiply_reduce_fusion.1
  352.3 10.7 %fusion.54 = bf16[160,2048]{1,0:T(8,128)(2,1)} fusion(bf16[1,4096,2048]{2,1,0:T(8,128)(2,1)} %param.18, bf16[160,2048]{1,0:T(8,128)(2,1)S(1)} %copy-done.9, f32[160]{0:T(256)S(1)} %add_rsqrt_fusion.2, f32[4096]{0:T(1024)S(1)} %bitcast.260, f32[160,4096]{1,0:T(8,128)S(1)} %copy.157, f32[160,9280]{1,0:T(8,128)} %get-tuple-element.46), kind=kOutput, calls=%fused_computation.71 | convolution fusion | flops 2690580480 | bytes 23347840 | tf_op jit(solution)/shard_map/dot_general | solution.py:102
  363.1 5.9 %collective-permute-start.3 = (bf16[160,2048]{1,0:T(8,128)(2,1)}, bf16[160,2048]{1,0:T(8,128)(2,1)S(1)}, u32[]{:S(2)}, u32[]{:S(2)}) collective-permute-start(bf16[160,2048]{1,0:T(8,128)(2,1)} %fusion.54), channel_id=1, source_target_pairs={{0,16},{16,32},{32,48},{48,64},{64,80},{80,96},{96,112},{1,17},{17... | collective-permute-start | bytes 1966088 | tf_op jit(solution)/shard_map/ppermute | solution.py:22
  369.0 0.9 slice.243
  369.9 1.3 collective-permute-start.4
  371.3 5.1 %add_convert_fusion = bf16[4,16,64,128]{3,2,1,0:T(8,128)(2,1)} fusion(bf16[4,16,64,128]{3,2,1,0:T(8,128)(2,1)} %bitcast.40, f32[4,16]{1,0:T(4,128)S(1)} %exp.107, bf16[160,4,128,1]{2,1,0,3:T(4,128)(2,1)S(1)} %bitcast.249, bf16[160,4,16,64]{0,3,2,1:T(8,128)(2,1)} %bitcast.216, f32[160,4,16]{0,2,1:T(8,128)S(1)} %bitcast.250), kind=kOutput, calls=%fused_computation.82 | convolution fusion | flops 1010040832 | bytes 3612928 | tf_op jit(solution)/shard_map/sghp,sgn->ghpn/dot_general | solution.py:85
  376.5 2.7 collective-permute-start.5
  379.1 15.9 %collective-permute-done.3 = bf16[160,2048]{1,0:T(8,128)(2,1)S(1)} collective-permute-done((bf16[160,2048]{1,0:T(8,128)(2,1)}, bf16[160,2048]{1,0:T(8,128)(2,1)S(1)}, u32[]{:S(2)}, u32[]{:S(2)}) %collective-permute-start.3) | collective-permute-done | bytes 655392 | tf_op jit(solution)/shard_map/ppermute | solution.py:22
  395.3 20.2 %fusion = f32[160,9280]{1,0:T(8,128)} fusion(bf16[1,2048,9280]{1,2,0:T(8,128)(2,1)} %all-gather.3.cloned.1.call-done, bf16[160,2048]{1,0:T(8,128)(2,1)S(1)} %get-tuple-element.11, f32[160]{0:T(256)S(1)} %add_rsqrt_fusion.1, f32[2048]{0:T(1024)S(1)} %bitcast.221), kind=kOutput, calls=%fused_computation | convolution fusion | flops 6083051520 | bytes 44614272 | tf_op jit(solution)/shard_map/dot_general | solution.py:98
  415.5 0.9 slice.252
  417.8 2.1 slice.336
  419.9 2.4 multiply_convert_fusion.6
  422.3 0.8 fusion.126
  423.1 0.6 exponential_multiply_fusion
  423.9 0.7 reshape.223
  424.6 0.7 reshape.222
  425.3 1.8 copy.167
  427.2 1.2 fusion.97
  428.4 4.1 fusion.14
  432.6 4.0 fusion.37
  436.6 5.2 %copy.162 = f32[160,4096]{1,0:T(8,128)} copy(f32[160,4096]{0,1:T(8,128)} %bitcast.208) | data formatting | bytes 5242880 | tf_op jit(solution)/shard_map/reshape | solution.py:79
  441.9 3.5 multiply_reduce_fusion
  445.5 10.7 %fusion.60 = bf16[1,160,2048]{2,1,0:T(8,128)(2,1)} fusion(bf16[1,4096,2048]{2,1,0:T(8,128)(2,1)} %param.18, bf16[160,2048]{1,0:T(8,128)(2,1)S(1)} %copy-done.7, f32[160]{0:T(256)S(1)} %add_rsqrt_fusion, f32[4096]{0:T(1024)S(1)} %bitcast.261, f32[160,4096]{1,0:T(8,128)S(1)} %copy-done, f32[160,9280]{1,0:T(8,128)} %fusion), kind=kOutput, calls=%fused_computation.73 | convolution fusion | flops 2690580480 | bytes 23347840 | tf_op jit(solution)/shard_map/dot_general | solution.py:102
  456.2 4.8 %multiply_add_fusion = f32[4,16,64,128]{3,2,1,0:T(8,128)} fusion(bf16[4,16,64,128]{3,2,1,0:T(8,128)(2,1)} %bitcast.56, f32[4,16]{1,0:T(4,128)S(1)} %exp.112, bf16[160,4,128,1]{2,1,0,3:T(4,128)(2,1)S(1)} %bitcast.222, bf16[160,4,16,64]{0,3,2,1:T(8,128)(2,1)S(1)} %bitcast.207, f32[160,4,16]{0,2,1:T(8,128)S(1)} %bitcast.240), kind=kOutput, calls=%fused_computation.81 | convolution fusion | flops 1009516544 | bytes 4661504 | tf_op jit(solution)/shard_map/sghp,sgn->ghpn/dot_general | solution.py:85
  (131 shorter events, 5.9 us)
Async XLA Ops:
  7.2 205.3 %all-gather.3.cloned.1.call-start = ((), (), s32[]{:S(2)}) async-start(), calls=%async_computation | async-start | bytes 40386560 | tf_op jit(solution)/shard_map/all_gather | solution.py:137
  14.7 218.3 %copy-start.18 = (f32[1,1,5120]{2,1,0:T(1,128)}, f32[1,1,5120]{2,1,0:T(1,128)S(1)}, u32[]{:S(2)}) copy-start(f32[1,1,5120]{2,1,0:T(1,128)S(1)} %get-tuple-element.30) | copy-start | bytes 61444
  14.7 218.3 %copy-start.20 = (f32[1,1,5120]{2,1,0:T(1,128)}, f32[1,1,5120]{2,1,0:T(1,128)S(1)}, u32[]{:S(2)}) copy-start(f32[1,1,5120]{2,1,0:T(1,128)S(1)} %get-tuple-element.31) | copy-start | bytes 61444
  14.7 218.3 %copy-start.22 = (f32[1,1,5120]{2,1,0:T(1,128)}, f32[1,1,5120]{2,1,0:T(1,128)S(1)}, u32[]{:S(2)}) copy-start(f32[1,1,5120]{2,1,0:T(1,128)S(1)} %get-tuple-element.32) | copy-start | bytes 61444
  14.7 218.3 %copy-start.24 = (f32[1,1,5120]{2,1,0:T(1,128)}, f32[1,1,5120]{2,1,0:T(1,128)S(1)}, u32[]{:S(2)}) copy-start(f32[1,1,5120]{2,1,0:T(1,128)S(1)} %get-tuple-element.33) | copy-start | bytes 61444
  232.7 3.2 copy-start.4
  232.7 0.7 copy-start.30
  232.7 0.8 copy-start.34
  237.0 9.1 %copy-start.1 = (f32[1,1,64,64,128]{4,3,2,1,0:T(8,128)S(1)}, f32[1,1,64,64,128]{4,3,2,1,0:T(8,128)}, u32[]{:S(2)}) copy-start(f32[1,1,64,64,128]{4,3,2,1,0:T(8,128)} %param.15) | copy-start | bytes 6291460
  240.4 4.2 copy-start.29
  246.0 3.0 copy-start.2
  246.0 3.0 copy-start.33
  246.0 3.0 copy-start.35
  258.4 2.7 copy-start.8
  258.4 2.7 copy-start.38
  261.1 18.8 %copy-start.14 = (bf16[160,512]{1,0:T(8,128)(2,1)S(1)}, bf16[160,512]{1,0:T(8,128)(2,1)}, u32[]{:S(2)}) copy-start(bf16[160,512]{1,0:T(8,128)(2,1)} %get-tuple-element.26) | copy-start | bytes 491524
  271.8 31.6 %copy-start.10 = (bf16[2,160,2048]{2,1,0:T(8,128)(2,1)S(1)}, bf16[2,160,2048]{2,1,0:T(8,128)(2,1)}, u32[]{:S(2)}) copy-start(bf16[2,160,2048]{2,1,0:T(8,128)(2,1)} %param.14) | copy-start | bytes 3932164
  271.8 31.6 %collective-permute-start = (bf16[160,2048]{1,0:T(8,128)(2,1)}, bf16[160,2048]{1,0:T(8,128)(2,1)S(1)}, u32[]{:S(2)}, u32[]{:S(2)}) collective-permute-start(bf16[160,2048]{1,0:T(8,128)(2,1)} %fusion.57), channel_id=1, source_target_pairs={{0,16},{16,32},{32,48},{48,64},{64,80},{80,96},{96,112},{1,17},{17... | collective-permute-start | bytes 1966088 | tf_op jit(solution)/shard_map/ppermute | solution.py:22
  277.9 49.9 %collective-permute-start.1 = (bf16[3,5120]{1,0:T(4,128)(2,1)S(1)}, bf16[3,5120]{1,0:T(4,128)(2,1)S(1)}, u32[]{:S(2)}, u32[]{:S(2)}) collective-permute-start(bf16[3,5120]{1,0:T(4,128)(2,1)S(1)} %slice.229), channel_id=1, source_target_pairs={{0,1},{1,2},{2,3},{3,4},{4,5},{5,6},{6,7},{7,8},{8,9},{9,10},{10,1... | collective-permute-start | bytes 92168 | tf_op jit(solution)/shard_map/ppermute | solution.py:22
  280.0 24.5 %copy-start.12 = (f32[1,2048]{1,0:T(1,128)S(1)}, f32[1,2048]{1,0:T(1,128)}, u32[]{:S(2)}) copy-start(f32[1,2048]{1,0:T(1,128)} %param.19) | copy-start | bytes 24580
  285.4 55.8 %collective-permute-start.2 = (bf16[64,64,128]{2,1,0:T(8,128)(2,1)}, bf16[64,64,128]{2,1,0:T(8,128)(2,1)}, u32[]{:S(2)}, u32[]{:S(2)}) collective-permute-start(bf16[64,64,128]{2,1,0:T(8,128)(2,1)} %bitcast.39), channel_id=1, source_target_pairs={{0,1},{1,2},{2,3},{3,4},{4,5},{5,6},{6,7},{7,8},{8,9},{9,10},{10,1... | collective-permute-start | bytes 3145736 | tf_op jit(solution)/shard_map/ppermute | solution.py:22
  304.5 21.8 %copy-start.36 = (f32[1,64]{1,0:T(1,128)S(1)}, f32[1,64]{1,0:T(1,128)}, u32[]{:S(2)}) copy-start(f32[1,64]{1,0:T(1,128)} %param.22) | copy-start | bytes 772
  304.5 21.8 %copy-start.37 = (f32[64]{0:T(128)S(1)}, f32[64]{0:T(128)}, u32[]{:S(2)}) copy-start(f32[64]{0:T(128)} %negate_bitcast_fusion) | copy-start | bytes 772
  325.0 5.2 %copy-start.5 = (bf16[160,9280]{1,0:T(8,128)(2,1)}, bf16[160,9280]{1,0:T(8,128)(2,1)S(1)}, u32[]{:S(2)}) copy-start(bf16[160,9280]{1,0:T(8,128)(2,1)S(1)} %get-tuple-element.45) | copy-start | bytes 8908804
  325.0 2.8 copy-start.19
  325.0 2.8 copy-start.21
  325.0 2.8 copy-start.23
  325.0 2.8 copy-start.25
  325.0 2.8 copy-start.31
  326.4 4.7 copy-start.28
  335.4 5.8 %copy-start.3 = (bf16[160,4096]{0,1:T(8,128)(2,1)}, bf16[160,4096]{0,1:T(8,128)(2,1)S(1)}, u32[]{:S(2)}) copy-start(bf16[160,4096]{0,1:T(8,128)(2,1)S(1)} %copy.166) | copy-start | bytes 3932164
  337.1 4.2 copy-start.17
  337.1 4.2 copy-start.26
  349.6 2.7 copy-start.9
  349.6 2.7 copy-start.39
  352.3 19.0 %copy-start.15 = (bf16[160,512]{1,0:T(8,128)(2,1)S(1)}, bf16[160,512]{1,0:T(8,128)(2,1)}, u32[]{:S(2)}) copy-start(bf16[160,512]{1,0:T(8,128)(2,1)} %get-tuple-element.22) | copy-start | bytes 491524
  352.3 19.0 %copy-start.32 = (f32[160,64]{0,1:T(8,128)S(1)}, f32[160,64]{0,1:T(8,128)}, u32[]{:S(2)}) copy-start(f32[160,64]{0,1:T(8,128)} %get-tuple-element.37) | copy-start | bytes 122884
  363.1 32.0 %copy-start.11 = (bf16[2,160,2048]{2,1,0:T(8,128)(2,1)S(1)}, bf16[2,160,2048]{2,1,0:T(8,128)(2,1)}, u32[]{:S(2)}) copy-start(bf16[2,160,2048]{2,1,0:T(8,128)(2,1)} %param.14) | copy-start | bytes 3932164
  363.1 31.9 %collective-permute-start.3 = (bf16[160,2048]{1,0:T(8,128)(2,1)}, bf16[160,2048]{1,0:T(8,128)(2,1)S(1)}, u32[]{:S(2)}, u32[]{:S(2)}) collective-permute-start(bf16[160,2048]{1,0:T(8,128)(2,1)} %fusion.54), channel_id=1, source_target_pairs={{0,16},{16,32},{32,48},{48,64},{64,80},{80,96},{96,112},{1,17},{17... | collective-permute-start | bytes 1966088 | tf_op jit(solution)/shard_map/ppermute | solution.py:22
  369.9 50.0 %collective-permute-start.4 = (bf16[3,5120]{1,0:T(4,128)(2,1)S(1)}, bf16[3,5120]{1,0:T(4,128)(2,1)S(1)}, u32[]{:S(2)}, u32[]{:S(2)}) collective-permute-start(bf16[3,5120]{1,0:T(4,128)(2,1)S(1)} %slice.243), channel_id=1, source_target_pairs={{0,1},{1,2},{2,3},{3,4},{4,5},{5,6},{6,7},{7,8},{8,9},{9,10},{10,1... | collective-permute-start | bytes 92168 | tf_op jit(solution)/shard_map/ppermute | solution.py:22
  376.5 56.1 %collective-permute-start.5 = (bf16[64,64,128]{2,1,0:T(8,128)(2,1)}, bf16[64,64,128]{2,1,0:T(8,128)(2,1)}, u32[]{:S(2)}, u32[]{:S(2)}) collective-permute-start(bf16[64,64,128]{2,1,0:T(8,128)(2,1)} %bitcast.55), channel_id=1, source_target_pairs={{0,1},{1,2},{2,3},{3,4},{4,5},{5,6},{6,7},{7,8},{8,9},{9,10},{10,1... | collective-permute-start | bytes 3145736 | tf_op jit(solution)/shard_map/ppermute | solution.py:22
  395.3 20.2 %copy-start.6 = (bf16[160,2048]{1,0:T(8,128)(2,1)}, bf16[160,2048]{1,0:T(8,128)(2,1)S(1)}, u32[]{:S(2)}) copy-start(bf16[160,2048]{1,0:T(8,128)(2,1)S(1)} %get-tuple-element.11) | copy-start | bytes 1966084
  416.6 6.5 %copy-start.27 = (f32[160,64]{0,1:T(8,128)}, f32[160,64]{0,1:T(8,128)S(1)}, u32[]{:S(2)}) copy-start(f32[160,64]{0,1:T(8,128)S(1)} %get-tuple-element.9) | copy-start | bytes 122884
  428.4 4.2 copy-start.16
  441.8 3.6 copy-start
  441.9 3.6 copy-start.7
  441.9 3.6 copy-start.40
  445.5 10.7 %copy-start.13 = (bf16[160,4,128]{2,1,0:T(4,128)(2,1)S(1)}, bf16[160,4,128]{2,1,0:T(4,128)(2,1)}, u32[]{:S(2)}) copy-start(bf16[160,4,128]{2,1,0:T(4,128)(2,1)} %reshape.223) | copy-start | bytes 491524
Sparse Core Ops, SparseCore 0:
  9.6 202.8 all-gather.2
where the time goes:
time: 477 us; the launch traced here: 468 us
  waiting for transfers between devices  228 us (48%)
  matrix products  138 us (29%)
  local copies, waits for them, and re-layouts  39 us (8%)
  other arithmetic  27.2 us (6%)
  starting transfers between devices  21.2 us (4%)
  between operations  15.1 us (3%)
    all_gather x1, waiting for transfers between devices, local(): in_full = lax.all_gather(in_shard, 'seq', axis=0, tiled=True)  198 us
    dot_general x3, matrix products, run_tile(): projected = jnp.dot(normed, in_full, preferred_element_type=jnp.float32)  60.9 us
    dot_general x3, matrix products, run_tile(): jnp.dot(mixed_norm, out_full, preferred_element_type=jnp.float32)  32.2 us
    ppermute x6, waiting for transfers between devices, from_behind(): return lax.ppermute(block, axis, route)  29.6 us
    ppermute x6, starting transfers between devices, from_behind(): return lax.ppermute(block, axis, route)  21.2 us
    dot_general x3, matrix products, mixer_core(): jnp.einsum('sghp,sgn->ghpn', scaled_input, write_map.astype(jnp.float32),...  15.4 us
    dot_general x3, matrix products, mixer_core(): jnp.einsum('ghts,sghp->tghp', weights, ssm_input, preferred_element_type=...  13.8 us
    reshape x3, local copies, waits for them, and re-layouts, mixer_core(): gated = combined.reshape(row_count, INNER) * jax.nn.silu(gate_branch)  13.3 us
  transfers between devices with their start and end apart: 7, of which 3 were waited for; matrix products, arithmetic and copies ran while one was open for 20% of the time, Pallas kernels for 0%

commit v1 on v0

v1 whole, which is shorter than its diff:
```python
import functools

import jax
import jax.numpy as jnp
from jax import lax
from jax.experimental import pallas as pl
from jax.experimental.pallas import tpu as pltpu
from jax.sharding import PartitionSpec as P

EPS = 1e-05
F32 = jnp.float32
BF16 = jnp.bfloat16
SEG = 160
WIDTH = 2048
HALF = 2048
CHUNK = 256
STEPS = HALF // CHUNK
PIECE = 512
PIECES = WIDTH // PIECE
MESH = pl.DeviceIdType.MESH
HIGHEST = lax.Precision.HIGHEST


def silu(v):
    half = 0.5 * v
    return half + half * jnp.tanh(half)


def dot(a, b):
    return jnp.dot(a, b, preferred_element_type=F32)


def by_rows(v, scale):
    blocks = [v[:, i : i + 128] * scale for i in range(0, v.shape[1], 128)]
    return blocks[0] if len(blocks) == 1 else jnp.concatenate(blocks, axis=1)


def lane_sums(v):
    total = v[:, :128]
    for i in range(128, v.shape[1], 128):
        total = total + v[:, i : i + 128]
    return total


def kernel(
    panels, feed, state_in, tail_in, w_in, w_dt, w_out, norm_gain, conv_w, conv_b, heads, skip, out_gain,
    panel_out, state_out,
    w_main, w_bc, w_o, hid, hg, ssq, rowscale, tails, s_in, s_loc, s_send, s_recv, s_stage, fd,
    convbuf, proj, b_all, c_all, score_a, score_b, ld_col, ld_row, st_row, e_ld, e_end, e_fin,
    gated, own_part, part_send, part_recv, sq_mine, sq_send, sq_recv, pan_send,
    g_send, g_recv, g_loc, l_sem, m_send, m_recv, p_send, p_recv, n_send, n_recv, r_send, r_recv,
    st_send, st_recv, f_send, f_recv, f_loc,
):
    layer = lax.axis_index("layer")
    seq = lax.axis_index("seq")
    c = lax.rem(seq, 2)
    m = lax.div(seq, 2)
    y = lax.rem(m, 4)
    z = lax.div(m, 4)
    oc = 1 - c
    yp = lax.rem(y + 1, 4)
    ym = lax.rem(y + 3, 4)
    y2 = lax.rem(y + 2, 4)
    oz = 1 - z

    def at(zz, yy, cc):
        return (layer, zz * 8 + yy * 2 + cc)

    sib = at(z, y, oc)
    to_yp = at(z, yp, c)
    to_ym = at(z, ym, c)
    to_z = at(oz, y, c)
    up = (lax.rem(layer + 1, 8), seq)
    down = (lax.rem(layer + 7, 8), seq)
    after = (layer, lax.rem(seq + 2, 16))
    before = (layer, lax.rem(seq + 14, 16))

    barrier = pltpu.get_barrier_semaphore()
    friends = (sib, to_yp, to_ym, to_z, up, down, after, before)
    for friend in friends:
        pl.semaphore_signal(barrier, inc=1, device_id=friend, device_id_type=MESH)
    pl.semaphore_wait(barrier, len(friends))

    def remote(src, dst, ss, rs, who):
        return pltpu.make_async_remote_copy(
            src_ref=src, dst_ref=dst, send_sem=ss, recv_sem=rs, device_id=who, device_id_type=MESH
        )

    def mult(v, by):
        return pl.multiple_of(v, by)

    own_rows = mult(m * 256 + c * 128, 128)
    sib_rows = mult(m * 256 + oc * 128, 128)

    def bc_first(cc):
        rows = pl.ds(own_rows, 128)
        return (
            (w_in.at[:, pl.ds(mult(8192 + cc * 256, 128), 256)], w_bc.at[rows, pl.ds(0, 256)]),
            (w_in.at[:, pl.ds(mult(8704 + cc * 256, 128), 256)], w_bc.at[rows, pl.ds(256, 256)]),
            (w_dt, w_bc.at[rows, pl.ds(512, 128)]),
        )

    def bc_landed():
        rows = pl.ds(sib_rows, 128)
        return (
            w_bc.at[rows, pl.ds(0, 256)],
            w_bc.at[rows, pl.ds(256, 256)],
            w_bc.at[rows, pl.ds(512, 128)],
        )

    bc_slots = (18, 19, 3)

    def main_first(q, cc):
        rows = pl.ds(own_rows, 128)
        return (
            (w_in.at[:, pl.ds(mult(4096 + cc * 2048 + q * 256, 128), 256)], w_main.at[q, rows, pl.ds(0, 256)]),
            (w_in.at[:, pl.ds(mult(cc * 2048 + q * 256, 128), 256)], w_main.at[q, rows, pl.ds(256, 256)]),
        )

    def main_landed(q):
        rows = pl.ds(sib_rows, 128)
        return (w_main.at[q, rows, pl.ds(0, 256)], w_main.at[q, rows, pl.ds(256, 256)])

    for (src, dst), slot in zip(bc_first(oc), bc_slots):
        remote(src, dst, g_send.at[8, slot], g_recv.at[8, slot], sib).start()
    for i, (src, dst) in enumerate(bc_first(c)):
        pltpu.make_async_copy(src, dst, g_loc.at[8, i]).start()

    @pl.loop(0, STEPS)
    def _(q):
        for i, (src, dst) in enumerate(main_first(q, oc)):
            remote(src, dst, g_send.at[q, 18 + i], g_recv.at[q, 18 + i], sib).start()
        for i, (src, dst) in enumerate(main_first(q, c)):
            pltpu.make_async_copy(src, dst, g_loc.at[q, i]).start()

    def bc_part(mm, half=None):
        if half is None:
            return w_bc.at[pl.ds(mult(mm * 256, 256), 256), :]
        return w_bc.at[pl.ds(mult(mm * 256 + half * 128, 128), 128), :]

    def x_part(q, mm, half=None):
        if half is None:
            return w_main.at[q, pl.ds(mult(mm * 256, 256), 256), pl.ds(0, 256)]
        return w_main.at[q, pl.ds(mult(mm * 256 + half * 128, 128), 128), pl.ds(0, 256)]

    def g_part(q, mm, half=None):
        if half is None:
            return w_main.at[q, pl.ds(mult(mm * 256, 256), 256), pl.ds(256, 256)]
        return w_main.at[q, pl.ds(mult(mm * 256 + half * 128, 128), 128), pl.ds(256, 256)]

    m_yp, m_ym, m_y2 = z * 4 + yp, z * 4 + ym, z * 4 + y2
    o_y, o_yp, o_ym, o_y2 = oz * 4 + y, oz * 4 + yp, oz * 4 + ym, oz * 4 + y2

    def push(part, q, slot, who):
        remote(part, part, g_send.at[q, slot], g_recv.at[q, slot], who).start()

    def arrived(part, q, slot):
        remote(part, part, g_send.at[q, slot], g_recv.at[q, slot], sib).wait_recv()

    def sent(part, q, slot):
        remote(part, part, g_send.at[q, slot], g_recv.at[q, slot], sib).wait_send()

    def first_x(part, q):
        push(part(m), q, 2, to_z)
        push(part(m), q, 0, to_yp)
        push(part(m), q, 1, to_ym)

    def first_g(part, q):
        push(part(m), q, 5, to_z)
        push(part(m), q, 3, to_yp)
        push(part(m), q, 4, to_ym)

    def second_x(part, q):
        arrived(part(o_y), q, 2)
        push(part(o_y), q, 6, to_yp)
        push(part(o_y), q, 7, to_ym)
        arrived(part(m_ym), q, 0)
        push(part(m_ym, 0), q, 8, to_yp)
        arrived(part(m_yp), q, 1)
        push(part(m_yp, 1), q, 9, to_ym)

    def second_g(part, q):
        arrived(part(m_ym), q, 3)
        push(part(m_ym), q, 11, to_z)
        push(part(m_ym, 0), q, 10, to_yp)
        arrived(part(m_yp), q, 4)
        push(part(m_yp), q, 13, to_z)
        push(part(m_yp, 1), q, 12, to_ym)
        arrived(part(o_y), q, 5)

    def third_x(part, q):
        arrived(part(o_ym), q, 6)
        push(part(o_ym, 0), q, 14, to_yp)
        arrived(part(o_yp), q, 7)
        push(part(o_yp, 1), q, 15, to_ym)
        arrived(part(m_y2, 0), q, 8)
        arrived(part(m_y2, 1), q, 9)

    def third_g(part, q):
        arrived(part(m_y2, 0), q, 10)
        push(part(m_y2, 0), q, 16, to_z)
        arrived(part(m_y2, 1), q, 12)
        push(part(m_y2, 1), q, 17, to_z)
        arrived(part(o_ym), q, 11)
        arrived(part(o_yp), q, 13)

    def last_x(part, q):
        arrived(part(o_y2, 0), q, 14)
        arrived(part(o_y2, 1), q, 15)

    def last_g(part, q):
        arrived(part(o_y2, 0), q, 16)
        arrived(part(o_y2, 1), q, 17)

    def sent_x(part, q):
        for slot in (0, 1, 2, 6, 7):
            sent(part(m), q, slot)
        for slot in (8, 9, 14, 15):
            sent(part(m, 0), q, slot)

    def sent_g(part, q):
        for slot in (3, 4, 5, 11, 13):
            sent(part(m), q, slot)
        for slot in (10, 12, 16, 17):
            sent(part(m, 0), q, slot)

    for (src, dst), slot, i in zip(bc_first(c), bc_slots, range(3)):
        pltpu.make_async_copy(src, dst, g_loc.at[8, i]).wait()
    for dst, slot in zip(bc_landed(), bc_slots):
        arrived(dst, 8, slot)
    first_x(bc_part, 8)

    @pl.loop(0, STEPS)
    def _(q):
        for i, (src, dst) in enumerate(main_first(q, c)):
            pltpu.make_async_copy(src, dst, g_loc.at[q, i]).wait()
        for i, dst in enumerate(main_landed(q)):
            arrived(dst, q, 18 + i)
        first_x(functools.partial(x_part, q), q)
        first_g(functools.partial(g_part, q), q)

    begin = (
        (panels, hid.at[0, c], 0),
        (tail_in, tails.at[0, c], 1),
        (state_in.at[pl.ds(mult(oc * HALF, HALF), HALF), :], s_in.at[c], 2),
    )
    for src, dst, i in begin:
        remote(src, dst, m_send.at[i], m_recv.at[i], sib).start()
    local = (
        (panels, hid.at[0, c]),
        (tail_in, tails.at[0, c]),
        (state_in.at[pl.ds(mult(c * HALF, HALF), HALF), :], s_in.at[c]),
        (w_out.at[pl.ds(mult(c * HALF, HALF), HALF), :], w_o),
        (feed, fd),
    )
    for i, (src, dst) in enumerate(local):
        pltpu.make_async_copy(src, dst, l_sem.at[i]).start()
    for i, (src, dst) in enumerate(local):
        pltpu.make_async_copy(src, dst, l_sem.at[i]).wait()
    for (src, dst, i), land in zip(begin, (hid.at[0, oc], tails.at[0, oc], s_in.at[oc])):
        remote(land, land, m_send.at[i], m_recv.at[i], sib).wait_recv()

    def ingest(t, tile, n):
        cols = pl.ds(mult(n * PIECE, PIECE), PIECE)
        rows = pl.ds(mult(tile * SEG, 32), SEG)
        h = hid[t, tile, :, cols].astype(F32)
        ssq[rows, :] += lane_sums(h * h)
        hg[rows, cols] = (h * norm_gain[:, cols]).astype(BF16)

    lane = lax.broadcasted_iota(jnp.int32, (SEG, 128), 1)
    row = lax.broadcasted_iota(jnp.int32, (SEG, 128), 0)

    def conv(width, tile_tail, fresh, weight, bias):
        convbuf[0:8, 0:width] = tile_tail
        convbuf[8 : 8 + SEG, 0:width] = fresh
        total = bias
        for k in range(4):
            total = total + convbuf[5 + k : 5 + k + SEG, 0:width] * weight[k : k + 1, :]
        return silu(total).astype(BF16)

    def tail_of(t, tile, cols):
        value = tails[t, tile, :, cols]
        if t > 0 and tile == 0:
            value = jnp.where(m > 0, value, 0.0)
        return value

    def keep_tail(t, tile, cols, width):
        if t < 2:
            tails[t + 1, 1 if tile == 0 else 2, :, cols] = convbuf[SEG : SEG + 8, 0:width]

    def prologue(t):
        total = jnp.sum(ssq[...], axis=1, keepdims=True)
        rowscale[...] = jnp.broadcast_to(lax.rsqrt(total * (1.0 / WIDTH) + EPS), (2 * SEG, 128))
        proj[:, 0:512] = dot(hg[...], w_bc[:, 0:512])
        logits = dot(hg[...], w_bc[:, 512:640])
        causal = lane <= row
        tri = (
            lax.broadcasted_iota(jnp.int32, (SEG, SEG), 1) <= lax.broadcasted_iota(jnp.int32, (SEG, SEG), 0)
        ).astype(F32)
        for tile in range(2):
            rows = slice(tile * SEG, (tile + 1) * SEG)
            scale = rowscale[rows, :]
            for which, base in ((0, 4096), (1, 4608)):
                cols = pl.ds(mult(base + c * 256, 128), 256)
                fresh = by_rows(proj[rows, which * 256 : which * 256 + 256], scale).astype(BF16).astype(F32)
                made = conv(256, tail_of(t, tile, cols), fresh, conv_w[:, cols], conv_b[:, cols])
                keep_tail(t, tile, cols, 256)
                target = b_all if which == 0 else c_all
                target[tile, 0] = made[:, 0:128]
                target[tile, 1] = made[:, 128:256]
            for g in range(2):
                scores = lax.dot_general(
                    c_all[tile, g], b_all[tile, g], (((1,), (1,)), ((), ())), preferred_element_type=F32
                )
                score_a[tile, g] = jnp.where(causal, scores[:, 0:128], 0.0)
                score_b[tile, g] = jnp.where(causal[0:32, 0:32], scores[128:SEG, 128:SEG], 0.0)
            v = logits[rows, :] * scale + heads[0:1, :]
            step = jnp.maximum(v, 0.0) + jnp.log1p(jnp.exp(-jnp.abs(v)))
            ld = jnp.dot(tri, -heads[1:2, :] * step, preferred_element_type=F32, precision=HIGHEST)
            last = ld[SEG - 1 : SEG, :]
            ld_col[tile] = ld
            ld_row[tile, :, 0:SEG] = ld.T
            st_row[tile, :, 0:SEG] = step.T
            e_ld[tile] = jnp.exp(ld).astype(BF16)
            e_end[tile] = (jnp.exp(last - ld) * step).astype(BF16)
            e_fin[tile] = jnp.broadcast_to(jnp.exp(last), (8, 128))

    def step_of(t, q):
        g = lax.div(q, 4)
        base = c * 32 + q * 4
        cols = pl.ds(mult(c * HALF + q * CHUNK, CHUNK), CHUNK)
        proj[...] = dot(hg[...], w_main[q])
        spread = (
            lax.broadcasted_iota(jnp.int32, (128, CHUNK), 0)
            == base + lax.div(lax.broadcasted_iota(jnp.int32, (128, CHUNK), 1), 64)
        ).astype(F32)
        spread16 = spread.astype(BF16)
        weight, bias = conv_w[:, cols], conv_b[:, cols]
        skip_now, gain_now = skip[:, cols], out_gain[:, cols]
        if t > 0:
            remote(s_recv.at[t - 1, q], s_recv.at[t - 1, q], st_send.at[t - 1, q], st_recv.at[t - 1, q], after).wait_recv()
        made = []
        for tile in range(2):
            rows = slice(tile * SEG, (tile + 1) * SEG)
            scale = rowscale[rows, :]
            fresh = by_rows(proj[rows, 0:CHUNK], scale).astype(BF16).astype(F32)
            x = conv(CHUNK, tail_of(t, tile, cols), fresh, weight, bias)
            keep_tail(t, tile, cols, CHUNK)
            if t == 0:
                state = s_in[tile, pl.ds(mult(q * CHUNK, CHUNK), CHUNK), :].T
            elif tile == 0:
                state = jnp.where(m > 0, s_recv[t - 1, q].astype(F32), 0.0)
            else:
                state = s_loc[q]
            ld = pltpu.roll(ld_col[tile], lax.rem(128 - base, 128), 1)
            sa, sb = score_a[tile, g], score_b[tile, g]
            pairs = []
            for pair in range(2):
                xp = x[:, pair * 128 : pair * 128 + 128]
                outs = []
                for i in range(2):
                    h = pair * 2 + i
                    col = jnp.broadcast_to(ld[:, h : h + 1], (SEG, 128))
                    ldr = ld_row[tile, pl.ds(base + h, 1), :]
                    str_ = st_row[tile, pl.ds(base + h, 1), :]
                    wa = sa * jnp.exp(jnp.minimum(col - ldr[:, 0:128], 0.0)) * str_[:, 0:128]
                    wb = sb * jnp.exp(jnp.minimum(col[128:SEG, 0:32] - ldr[:, 128:SEG], 0.0)) * str_[:, 128:SEG]
                    oa = dot(wa.astype(BF16), xp[0:128])
                    ob = dot(wb.astype(BF16), xp[128:SEG])
                    outs.append(jnp.concatenate([oa[0:128], oa[128:SEG] + ob], axis=0))
                pairs.append(jnp.where(lane < 64, outs[0], outs[1]))
            mixed = jnp.concatenate(pairs, axis=1)
            carried = dot(c_all[tile, g], state.astype(BF16)) * dot(e_ld[tile], spread16)
            wide = x.astype(F32)
            combined = mixed + carried + skip_now * wide
            out = combined * silu(by_rows(proj[rows, CHUNK : 2 * CHUNK], scale))
            sq_mine[rows, :] += lane_sums(out * out)
            gated[rows, pl.ds(mult(q * CHUNK, CHUNK), CHUNK)] = (out * gain_now).astype(BF16)
            scaled = (wide * dot(e_end[tile], spread16)).astype(BF16)
            grown = lax.dot_general(
                b_all[tile, g], scaled, (((0,), (0,)), ((), ())), preferred_element_type=F32
            )
            fade = jnp.dot(e_fin[tile], spread, preferred_element_type=F32, precision=HIGHEST)
            made.append(fade[0:1, :] * state + grown)
        if t < 2:
            s_loc[q] = made[0]
            s_send[t, q] = made[1].astype(BF16)
            remote(s_send.at[t, q], s_recv.at[t, q], st_send.at[t, q], st_recv.at[t, q], after).start()
        else:
            s_stage[0, q] = made[0].T
            s_stage[1, q] = made[1].T
            place = state_out.at[pl.ds(mult(c * HALF + q * CHUNK, CHUNK), CHUNK), :]
            pltpu.make_async_copy(s_stage.at[c, q], place, f_loc.at[q]).start()
            remote(s_stage.at[oc, q], place, f_send.at[q], f_recv.at[q], sib).start()

    own = pl.ds(mult(c * SEG, 32), SEG)
    other = pl.ds(mult(oc * SEG, 32), SEG)

    def project_out(t, n):
        cols = pl.ds(mult(n * PIECE, PIECE), PIECE)
        proj[...] = dot(gated[...], w_o[:, cols])
        part_send[t, n] = proj[other, :].astype(BF16)
        own_part[n] = proj[own, :]
        remote(part_send.at[t, n], part_recv.at[t, n], p_send.at[t, n], p_recv.at[t, n], sib).start()

    def finish(t, n, scale):
        cols = pl.ds(mult(n * PIECE, PIECE), PIECE)
        remote(part_recv.at[t, n], part_recv.at[t, n], p_send.at[t, n], p_recv.at[t, n], sib).wait_recv()
        whole = own_part[n] + part_recv[t, n].astype(F32)
        panel = (hid[t, c, :, cols].astype(F32) + by_rows(whole, scale)).astype(BF16)
        if t < 2:
            pan_send[t, :, cols] = jnp.where(layer == 7, fd[t, :, cols].astype(F32), panel.astype(F32)).astype(BF16)
            remote(
                pan_send.at[t, :, cols], hid.at[t + 1, c, :, cols], n_send.at[t, n], n_recv.at[t, n], up
            ).start()
        else:
            panel_out[:, cols] = panel

    for t in range(3):
        ssq[...] = jnp.zeros((2 * SEG, 128), F32)
        sq_mine[...] = jnp.zeros((2 * SEG, 128), F32)
        if t == 0:

            @pl.loop(0, 2 * PIECES)
            def _(i):
                ingest(0, lax.rem(i, 2), lax.div(i, 2))

            second_x(bc_part, 8)

            @pl.loop(0, STEPS)
            def _(q):
                second_x(functools.partial(x_part, q), q)
                second_g(functools.partial(g_part, q), q)

            third_x(bc_part, 8)

            @pl.loop(0, STEPS)
            def _(q):
                third_x(functools.partial(x_part, q), q)
                third_g(functools.partial(g_part, q), q)

            last_x(bc_part, 8)
        else:

            @pl.loop(0, PIECES)
            def _(n):
                part = hid.at[t, c, :, pl.ds(mult(n * PIECE, PIECE), PIECE)]
                remote(part, part, n_send.at[t - 1, n], n_recv.at[t - 1, n], up).wait_recv()
                remote(part, part, r_send.at[t - 1, n], r_recv.at[t - 1, n], sib).start()
                ingest(t, c, n)

            @pl.loop(0, PIECES)
            def _(n):
                part = hid.at[t, oc, :, pl.ds(mult(n * PIECE, PIECE), PIECE)]
                remote(part, part, r_send.at[t - 1, n], r_recv.at[t - 1, n], sib).wait_recv()
                ingest(t, oc, n)

            remote(tails.at[t, 0], tails.at[t, 0], m_send.at[2 + t], m_recv.at[2 + t], after).wait_recv()
        prologue(t)

        @pl.loop(0, STEPS)
        def _(q):
            if t == 0:
                last_x(functools.partial(x_part, q), q)
                last_g(functools.partial(g_part, q), q)
            step_of(t, q)

        if t < 2:
            remote(tails.at[t + 1, 2], tails.at[t + 1, 0], m_send.at[3 + t], m_recv.at[3 + t], after).start()
        sq_send[t] = sq_mine[other, :]
        remote(sq_send.at[t], sq_recv.at[t], m_send.at[5 + t], m_recv.at[5 + t], sib).start()
        project_out(t, 0)
        remote(sq_recv.at[t], sq_recv.at[t], m_send.at[5 + t], m_recv.at[5 + t], sib).wait_recv()
        squares = jnp.sum(sq_mine[own, :] + sq_recv[t], axis=1, keepdims=True)
        rowscale[0:SEG, :] = jnp.broadcast_to(lax.rsqrt(squares * (1.0 / 4096) + EPS), (SEG, 128))

        @pl.loop(1, PIECES)
        def _(n):
            project_out(t, n)
            finish(t, n - 1, rowscale[0:SEG, :])

        finish(t, PIECES - 1, rowscale[0:SEG, :])

    for i, slot in enumerate(bc_slots):
        sent(bc_landed()[i], 8, slot)
    sent_x(bc_part, 8)

    @pl.loop(0, STEPS)
    def _(q):
        for i, dst in enumerate(main_landed(q)):
            sent(dst, q, 18 + i)
        sent_x(functools.partial(x_part, q), q)
        sent_g(functools.partial(g_part, q), q)
        place = state_out.at[pl.ds(mult(c * HALF + q * CHUNK, CHUNK), CHUNK), :]
        land = state_out.at[pl.ds(mult(oc * HALF + q * CHUNK, CHUNK), CHUNK), :]
        pltpu.make_async_copy(s_stage.at[c, q], place, f_loc.at[q]).wait()
        remote(s_stage.at[oc, q], land, f_send.at[q], f_recv.at[q], sib).wait()
        for t in range(2):
            remote(s_send.at[t, q], s_recv.at[t, q], st_send.at[t, q], st_recv.at[t, q], after).wait_send()

    for src, dst, i in begin:
        remote(src, dst, m_send.at[i], m_recv.at[i], sib).wait_send()
    for t in range(2):
        remote(tails.at[t + 1, 2], tails.at[t + 1, 0], m_send.at[3 + t], m_recv.at[3 + t], after).wait_send()
    for t in range(3):
        remote(sq_send.at[t], sq_recv.at[t], m_send.at[5 + t], m_recv.at[5 + t], sib).wait_send()

    @pl.loop(0, PIECES)
    def _(n):
        cols = pl.ds(mult(n * PIECE, PIECE), PIECE)
        for t in range(3):
            remote(part_send.at[t, n], part_recv.at[t, n], p_send.at[t, n], p_recv.at[t, n], sib).wait_send()
        for t in range(2):
            part = hid.at[t + 1, c, :, cols]
            remote(pan_send.at[t, :, cols], part, n_send.at[t, n], n_recv.at[t, n], up).wait_send()
            remote(part, part, r_send.at[t, n], r_recv.at[t, n], sib).wait_send()


def local(
    panels, feed, ssm_state, conv_state, w_in, w_out, norm_gain, conv_weight, conv_bias,
    dt_bias, decay_rate, skip_gain, out_gain,
):
    tail = jnp.pad(conv_state[0, 0].astype(F32), ((5, 0), (0, 0)))
    w_dt = jnp.pad(w_in[0, :, 9216:], ((0, 0), (0, 64)))
    heads = jnp.pad(jnp.concatenate([dt_bias, decay_rate], axis=0), ((0, 6), (0, 64)))
    skip = jnp.repeat(skip_gain, 64, axis=1)
    any_ = pl.BlockSpec(memory_space=pl.ANY)
    vmem = pl.BlockSpec(memory_space=pltpu.VMEM)
    dma = pltpu.SemaphoreType.DMA
    scratch = [
        pltpu.VMEM((STEPS, 2048, 512), BF16),
        pltpu.VMEM((2048, 640), BF16),
        pltpu.VMEM((HALF, WIDTH), BF16),
        pltpu.VMEM((3, 2, SEG, WIDTH), BF16),
        pltpu.VMEM((2 * SEG, WIDTH), BF16),
        pltpu.VMEM((2 * SEG, 128), F32),
        pltpu.VMEM((2 * SEG, 128), F32),
        pltpu.VMEM((3, 3, 8, 5120), F32),
        pltpu.VMEM((2, HALF, 128), F32),
        pltpu.VMEM((STEPS, 128, CHUNK), F32),
        pltpu.VMEM((2, STEPS, 128, CHUNK), BF16),
        pltpu.VMEM((2, STEPS, 128, CHUNK), BF16),
        pltpu.VMEM((2, STEPS, CHUNK, 128), F32),
        pltpu.VMEM((2, SEG, WIDTH), BF16),
        pltpu.VMEM((SEG + 8, 256), F32),
        pltpu.VMEM((2 * SEG, 512), F32),
        pltpu.VMEM((2, 2, SEG, 128), BF16),
        pltpu.VMEM((2, 2, SEG, 128), BF16),
        pltpu.VMEM((2, 2, SEG, 128), F32),
        pltpu.VMEM((2, 2, 32, 32), F32),
        pltpu.VMEM((2, SEG, 128), F32),
        pltpu.VMEM((2, 128, 256), F32),
        pltpu.VMEM((2, 128, 256), F32),
        pltpu.VMEM((2, SEG, 128), BF16),
        pltpu.VMEM((2, SEG, 128), BF16),
        pltpu.VMEM((2, 8, 128), F32),
        pltpu.VMEM((2 * SEG, HALF), BF16),
        pltpu.VMEM((PIECES, SEG, PIECE), F32),
        pltpu.VMEM((3, PIECES, SEG, PIECE), BF16),
        pltpu.VMEM((3, PIECES, SEG, PIECE), BF16),
        pltpu.VMEM((2 * SEG, 128), F32),
        pltpu.VMEM((3, SEG, 128), F32),
        pltpu.VMEM((3, SEG, 128), F32),
        pltpu.VMEM((2, SEG, WIDTH), BF16),
        dma((9, 20)), dma((9, 20)), dma((9, 3)), dma((5,)), dma((8,)), dma((8,)),
        dma((3, PIECES)), dma((3, PIECES)), dma((2, PIECES)), dma((2, PIECES)), dma((2, PIECES)), dma((2, PIECES)),
        dma((2, STEPS)), dma((2, STEPS)), dma((STEPS,)), dma((STEPS,)), dma((STEPS,)),
    ]
    panel, state = pl.pallas_call(
        kernel,
        out_shape=(
            jax.ShapeDtypeStruct((SEG, WIDTH), BF16),
            jax.ShapeDtypeStruct((4096, 128), F32),
        ),
        in_specs=[any_, any_, any_, any_, any_, any_, any_] + [vmem] * 6,
        out_specs=(vmem, any_),
        scratch_shapes=scratch,
        compiler_params=pltpu.CompilerParams(
            collective_id=0, has_side_effects=True, vmem_limit_bytes=60 * 1024 * 1024
        ),
        cost_estimate=pl.CostEstimate(flops=28_000_000_000, bytes_accessed=60_000_000, transcendentals=20_000_000),
    )(
        panels[0], feed, ssm_state.reshape(4096, 128), tail, w_in[0], w_dt, w_out[0],
        norm_gain, conv_weight[0], conv_bias, heads, skip, out_gain,
    )
    return (panel[None], state.reshape(1, 1, 64, 64, 128))


def solution(mesh):
    return jax.shard_map(
        local,
        mesh=mesh,
        in_specs=(
            P("layer", "seq", None),
            P(None, "seq", None),
            P("layer", "seq", None, None, None),
            P("layer", "seq", None, None),
            P("layer", "seq", None),
            P("layer", None, None),
            P("layer", None),
            P("layer", None, None),
            P("layer", None),
            P("layer", None),
            P("layer", None),
            P("layer", None),
            P("layer", None),
        ),
        out_specs=(P("layer", "seq", None), P("layer", "seq", None, None, None)),
        check_vma=False,
    )
```

time: 477 us -> 251 us (0.53); the launches traced: 468 us -> 249 us
  Pallas kernels: 0 us -> 235 us
  waiting for transfers between devices: 228 us -> 0 us
  matrix products: 138 us -> 0 us
  local copies, waits for them, and re-layouts: 39 us -> 11.1 us
  other arithmetic: 27.2 us -> 2.75 us
  starting transfers between devices: 21.2 us -> 0 us
  between operations: 15.1 us -> 0.67 us
    pallas_call x0 -> x1, Pallas kernels: none -> 235 us  [local(): pl.pallas_call(kernel, out_shape=(jax.ShapeDtypeStruct((SEG, WIDTH), BF16...]
    all_gather x1 -> x0, waiting for transfers between devices: 198 us -> none  [local(): in_full = lax.all_gather(in_shard, 'seq', axis=0, tiled=True)]
    dot_general x18 -> x0, matrix products: 138 us -> none  [the longest x3 60.9 us: run_tile(): projected = jnp.dot(normed, in_full, preferred_element_type=jnp.float32)]
    ppermute x6 -> x0, waiting for transfers between devices: 29.6 us -> none  [from_behind(): return lax.ppermute(block, axis, route)]
    reshape x13 -> x0, local copies, waits for them, and re-layouts: 24.1 us -> none  [the longest x3 13.3 us: mixer_core(): gated = combined.reshape(row_count, INNER) * jax.nn.silu(gate_branch)]
    ppermute x6 -> x0, starting transfers between devices: 21.2 us -> none  [from_behind(): return lax.ppermute(block, axis, route)]
    slice x18 -> x0, local copies, waits for them, and re-layouts: 12 us -> none  [the longest x3 3.13 us: mixer_core(): step_logit = projected[:, INNER + CONV_CH:]]
    reduce_sum x6 -> x0, other arithmetic: 11.5 us -> none  [rms_scale(): jnp.mean(values * values, axis=-1, keepdims=True) + EPS]
  transfers between devices with their start and end apart: 7 -> 0, of which waited for: 3 -> 0; matrix products, arithmetic and copies ran while one was open for 20% -> 0% of each run, Pallas kernels for 0% -> 0%
where the time goes in v1:
time: 251 us; the launch traced here: 249 us
  Pallas kernels  235 us (94%)
  local copies, waits for them, and re-layouts  11.1 us (4%)
  other arithmetic  2.75 us (1%)
    pallas_call x1, Pallas kernels, local(): pl.pallas_call(kernel, out_shape=(jax.ShapeDtypeStruct((SEG, WIDTH), BF16...  235 us
    unnamed x5, local copies, waits for them, and re-layouts  9 us

profile of v1, /device:TPU:2, one launch (start us, length us, event | category | flops | bytes accessed | tf_op | source)
XLA Modules:
  0.0 249.2 jit_solution(5287709728654602375)
XLA Ops:
  0.6 1.3 select_maximum_fusion.heads
  1.9 0.7 broadcast_in_dim.8
  2.6 0.7 broadcast_in_dim.9.skip
  3.3 1.5 pad_convert_fusion.tail_in
  4.8 3.1 %copy.15 = bf16[1,128,9280]{2,1,0:T(8,128)(2,1)S(1)} copy(bf16[1,128,9280]{1,2,0:T(8,128)(2,1)} %param.17) | data formatting | bytes 4751360 | tf_op args[4]
  7.9 0.0 copy-start
  7.9 0.7 pad.16.w_dt
  8.6 0.7 copy-done
  9.4 234.7 %shard_map.143 = (bf16[160,2048]{1,0:T(8,128)(2,1)}, f32[4096,128]{1,0:T(8,128)}) custom-call(bf16[160,2048]{1,0:T(8,128)(2,1)} %bitcast.18, bf16[2,160,2048]{2,1,0:T(8,128)(2,1)} %feed.1, f32[4096,128]{1,0:T(8,128)} %bitcast.17, f32[8,5120]{1,0:T(8,128)} %pad_convert_fusion.tail_in, bf16[128,9280]{1,0:T(8,128)(2,1)} %bitcast.11, ...), custom_call_target="tpu_custom_call" | custom-call | flops 28000000000 | bytes 60000000 | tf_op jit(solution)/shard_map/pallas_call | solution.py:569
  244.0 2.0 copy.19
  246.0 3.2 %copy.20 = f32[1,1,64,64,128]{4,3,2,1,0:T(8,128)} copy(f32[1,1,64,64,128]{4,3,2,1,0:T(8,128)} %bitcast.12) | data formatting | bytes 4194304
  (1 shorter events, 0.0 us)
Async XLA Ops:
  7.9 1.5 copy-start

commit v2 on v1

--- a/solution.py
+++ b/solution.py
@@ -8,6 +8,7 @@
 from jax.sharding import PartitionSpec as P
 
 EPS = 1e-05
+LOG2E = 1.4426950408889634
 F32 = jnp.float32
 BF16 = jnp.bfloat16
 SEG = 160
@@ -21,8 +22,7 @@
 HIGHEST = lax.Precision.HIGHEST
 
 
-def silu(v):
-    half = 0.5 * v
+def silu_of_half(half):
     return half + half * jnp.tanh(half)
 
 
@@ -43,12 +43,13 @@
 
 
 def kernel(
-    panels, feed, state_in, tail_in, w_in, w_dt, w_out, norm_gain, conv_w, conv_b, heads, skip, out_gain,
+    panels, feed, state_in, w_in, w_out, tail_in, norm_gain, conv_w, conv_b, dt_bias, decay_rate, skip_gain, out_gain,
     panel_out, state_out,
+    w_rows, w_cut, bc_cut, heads,
     w_main, w_bc, w_o, hid, hg, ssq, rowscale, tails, s_in, s_loc, s_send, s_recv, s_stage, fd,
-    convbuf, proj, b_all, c_all, score_a, score_b, ld_col, ld_row, st_row, e_ld, e_end, e_fin,
+    convbuf, proj, spread_out, b_all, c_all, score_a, score_b, ld_col, ld_row, e_all, e_fin,
     gated, own_part, part_send, part_recv, sq_mine, sq_send, sq_recv, pan_send,
-    g_send, g_recv, g_loc, l_sem, m_send, m_recv, p_send, p_recv, n_send, n_recv, r_send, r_recv,
+    g_send, g_recv, l_sem, m_send, m_recv, p_send, p_recv, n_send, n_recv, r_send, r_recv,
     st_send, st_recv, f_send, f_recv, f_loc,
 ):
     layer = lax.axis_index("layer")
@@ -75,10 +76,35 @@
     after = (layer, lax.rem(seq + 2, 16))
     before = (layer, lax.rem(seq + 14, 16))
 
+    def mult(v, by):
+        return pl.multiple_of(v, by)
+
+    local = (
+        (w_in.at[pl.ds(8192, 1088), :], w_rows.at[pl.ds(8192, 1088), :]),
+        (w_in.at[pl.ds(4096, 4096), :], w_rows.at[pl.ds(4096, 4096), :]),
+        (w_in.at[pl.ds(0, 4096), :], w_rows.at[pl.ds(0, 4096), :]),
+        (panels, hid.at[0, c]),
+        (state_in.at[pl.ds(mult(c * HALF, HALF), HALF), :], s_in.at[c]),
+        (w_out.at[pl.ds(mult(c * HALF, HALF), HALF), :], w_o),
+        (feed, fd),
+    )
+    for i, (src, dst) in enumerate(local[:3]):
+        pltpu.make_async_copy(src, dst, l_sem.at[i]).start()
+
     barrier = pltpu.get_barrier_semaphore()
     friends = (sib, to_yp, to_ym, to_z, up, down, after, before)
     for friend in friends:
         pl.semaphore_signal(barrier, inc=1, device_id=friend, device_id_type=MESH)
+
+    heads[...] = jnp.zeros((8, 128), F32)
+    heads[0:1, 0:64] = dt_bias[...]
+    heads[1:2, 0:64] = decay_rate[...]
+    heads[2:3, 0:64] = skip_gain[...]
+    tails[0, c, 0:8, :] = jnp.zeros((8, 5120), F32)
+    tails[0, c, 5:8, :] = tail_in[...].astype(F32)
+
+    for i, (src, dst) in enumerate(local[:3]):
+        pltpu.make_async_copy(src, dst, l_sem.at[i]).wait()
     pl.semaphore_wait(barrier, len(friends))
 
     def remote(src, dst, ss, rs, who):
@@ -86,52 +112,34 @@
             src_ref=src, dst_ref=dst, send_sem=ss, recv_sem=rs, device_id=who, device_id_type=MESH
         )
 
-    def mult(v, by):
-        return pl.multiple_of(v, by)
-
     own_rows = mult(m * 256 + c * 128, 128)
     sib_rows = mult(m * 256 + oc * 128, 128)
 
-    def bc_first(cc):
+    def turned(start, size):
+        return w_rows[pl.ds(mult(start, 64), size), :].T
+
+    def bc_prepare():
+        dt = jnp.concatenate([turned(9216, 64), jnp.zeros((128, 64), BF16)], axis=1)
         rows = pl.ds(own_rows, 128)
-        return (
-            (w_in.at[:, pl.ds(mult(8192 + cc * 256, 128), 256)], w_bc.at[rows, pl.ds(0, 256)]),
-            (w_in.at[:, pl.ds(mult(8704 + cc * 256, 128), 256)], w_bc.at[rows, pl.ds(256, 256)]),
-            (w_dt, w_bc.at[rows, pl.ds(512, 128)]),
-        )
+        for cc, target, where in ((c, w_bc, rows), (oc, bc_cut, slice(0, 128))):
+            target[where, 0:256] = turned(8192 + cc * 256, 256)
+            target[where, 256:512] = turned(8704 + cc * 256, 256)
+            target[where, 512:640] = dt
+        remote(bc_cut, w_bc.at[rows, :], g_send.at[8, 18], g_recv.at[8, 18], sib).start()
+
+    def main_prepare(q):
+        rows = pl.ds(own_rows, 128)
+        w_main[q, rows, 0:256] = turned(4096 + c * 2048 + q * 256, 256)
+        w_main[q, rows, 256:512] = turned(c * 2048 + q * 256, 256)
+        w_cut[q, :, 0:256] = turned(4096 + oc * 2048 + q * 256, 256)
+        w_cut[q, :, 256:512] = turned(oc * 2048 + q * 256, 256)
+        remote(w_cut.at[q], w_main.at[q, rows, :], g_send.at[q, 18], g_recv.at[q, 18], sib).start()
 
     def bc_landed():
-        rows = pl.ds(sib_rows, 128)
-        return (
-            w_bc.at[rows, pl.ds(0, 256)],
-            w_bc.at[rows, pl.ds(256, 256)],
-            w_bc.at[rows, pl.ds(512, 128)],
-        )
-
-    bc_slots = (18, 19, 3)
-
-    def main_first(q, cc):
-        rows = pl.ds(own_rows, 128)
-        return (
-            (w_in.at[:, pl.ds(mult(4096 + cc * 2048 + q * 256, 128), 256)], w_main.at[q, rows, pl.ds(0, 256)]),
-            (w_in.at[:, pl.ds(mult(cc * 2048 + q * 256, 128), 256)], w_main.at[q, rows, pl.ds(256, 256)]),
-        )
+        return w_bc.at[pl.ds(sib_rows, 128), :]
 
     def main_landed(q):
-        rows = pl.ds(sib_rows, 128)
-        return (w_main.at[q, rows, pl.ds(0, 256)], w_main.at[q, rows, pl.ds(256, 256)])
-
-    for (src, dst), slot in zip(bc_first(oc), bc_slots):
-        remote(src, dst, g_send.at[8, slot], g_recv.at[8, slot], sib).start()
-    for i, (src, dst) in enumerate(bc_first(c)):
-        pltpu.make_async_copy(src, dst, g_loc.at[8, i]).start()
-
-    @pl.loop(0, STEPS)
-    def _(q):
-        for i, (src, dst) in enumerate(main_first(q, oc)):
-            remote(src, dst, g_send.at[q, 18 + i], g_recv.at[q, 18 + i], sib).start()
-        for i, (src, dst) in enumerate(main_first(q, c)):
-            pltpu.make_async_copy(src, dst, g_loc.at[q, i]).start()
+        return w_main.at[q, pl.ds(sib_rows, 128), :]
 
     def bc_part(mm, half=None):
         if half is None:
@@ -224,39 +232,32 @@
         for slot in (10, 12, 16, 17):
             sent(part(m, 0), q, slot)
 
-    for (src, dst), slot, i in zip(bc_first(c), bc_slots, range(3)):
-        pltpu.make_async_copy(src, dst, g_loc.at[8, i]).wait()
-    for dst, slot in zip(bc_landed(), bc_slots):
-        arrived(dst, 8, slot)
+    bc_prepare()
+    main_prepare(0)
+    arrived(bc_landed(), 8, 18)
     first_x(bc_part, 8)
 
     @pl.loop(0, STEPS)
     def _(q):
-        for i, (src, dst) in enumerate(main_first(q, c)):
-            pltpu.make_async_copy(src, dst, g_loc.at[q, i]).wait()
-        for i, dst in enumerate(main_landed(q)):
-            arrived(dst, q, 18 + i)
+        @pl.when(q < STEPS - 1)
+        def _():
+            main_prepare(q + 1)
+
+        arrived(main_landed(q), q, 18)
         first_x(functools.partial(x_part, q), q)
         first_g(functools.partial(g_part, q), q)
 
     begin = (
         (panels, hid.at[0, c], 0),
-        (tail_in, tails.at[0, c], 1),
+        (tails.at[0, c], tails.at[0, c], 1),
         (state_in.at[pl.ds(mult(oc * HALF, HALF), HALF), :], s_in.at[c], 2),
     )
     for src, dst, i in begin:
         remote(src, dst, m_send.at[i], m_recv.at[i], sib).start()
-    local = (
-        (panels, hid.at[0, c]),
-        (tail_in, tails.at[0, c]),
-        (state_in.at[pl.ds(mult(c * HALF, HALF), HALF), :], s_in.at[c]),
-        (w_out.at[pl.ds(mult(c * HALF, HALF), HALF), :], w_o),
-        (feed, fd),
-    )
-    for i, (src, dst) in enumerate(local):
-        pltpu.make_async_copy(src, dst, l_sem.at[i]).start()
-    for i, (src, dst) in enumerate(local):
-        pltpu.make_async_copy(src, dst, l_sem.at[i]).wait()
+    for i, (src, dst) in enumerate(local[3:]):
+        pltpu.make_async_copy(src, dst, l_sem.at[3 + i]).start()
+    for i, (src, dst) in enumerate(local[3:]):
+        pltpu.make_async_copy(src, dst, l_sem.at[3 + i]).wait()
     for (src, dst, i), land in zip(begin, (hid.at[0, oc], tails.at[0, oc], s_in.at[oc])):
         remote(land, land, m_send.at[i], m_recv.at[i], sib).wait_recv()
 
@@ -270,13 +271,13 @@
     lane = lax.broadcasted_iota(jnp.int32, (SEG, 128), 1)
     row = lax.broadcasted_iota(jnp.int32, (SEG, 128), 0)
 
-    def conv(width, tile_tail, fresh, weight, bias):
-        convbuf[0:8, 0:width] = tile_tail
-        convbuf[8 : 8 + SEG, 0:width] = fresh
+    def conv(slot, tile_tail, fresh, weight, bias):
+        convbuf[slot, 0:8, :] = tile_tail
+        convbuf[slot, 8 : 8 + SEG, :] = fresh
         total = bias
         for k in range(4):
-            total = total + convbuf[5 + k : 5 + k + SEG, 0:width] * weight[k : k + 1, :]
-        return silu(total).astype(BF16)
+            total = total + convbuf[slot, 5 + k : 5 + k + SEG, :] * weight[k : k + 1, :]
+        return silu_of_half(total).astype(BF16)
 
     def tail_of(t, tile, cols):
         value = tails[t, tile, :, cols]
@@ -284,14 +285,14 @@
             value = jnp.where(m > 0, value, 0.0)
         return value
 
-    def keep_tail(t, tile, cols, width):
+    def keep_tail(t, tile, cols, slot):
         if t < 2:
-            tails[t + 1, 1 if tile == 0 else 2, :, cols] = convbuf[SEG : SEG + 8, 0:width]
+            tails[t + 1, 1 if tile == 0 else 2, :, cols] = convbuf[slot, SEG : SEG + 8, :]
 
     def prologue(t):
         total = jnp.sum(ssq[...], axis=1, keepdims=True)
         rowscale[...] = jnp.broadcast_to(lax.rsqrt(total * (1.0 / WIDTH) + EPS), (2 * SEG, 128))
-        proj[:, 0:512] = dot(hg[...], w_bc[:, 0:512])
+        proj[...] = dot(hg[...], w_bc[:, 0:512])
         logits = dot(hg[...], w_bc[:, 512:640])
         causal = lane <= row
         tri = (
@@ -300,14 +301,15 @@
         for tile in range(2):
             rows = slice(tile * SEG, (tile + 1) * SEG)
             scale = rowscale[rows, :]
-            for which, base in ((0, 4096), (1, 4608)):
-                cols = pl.ds(mult(base + c * 256, 128), 256)
-                fresh = by_rows(proj[rows, which * 256 : which * 256 + 256], scale).astype(BF16).astype(F32)
-                made = conv(256, tail_of(t, tile, cols), fresh, conv_w[:, cols], conv_b[:, cols])
-                keep_tail(t, tile, cols, 256)
-                target = b_all if which == 0 else c_all
-                target[tile, 0] = made[:, 0:128]
-                target[tile, 1] = made[:, 128:256]
+            for block in range(4):
+                slot = block % 2
+                base = 4096 if block < 2 else 4608
+                cols = pl.ds(mult(base + c * 256 + slot * 128, 128), 128)
+                fresh = proj[rows, block * 128 : block * 128 + 128] * scale
+                made = conv(tile * 2 + slot, tail_of(t, tile, cols), fresh, 0.5 * conv_w[:, cols], 0.5 * conv_b[:, cols])
+                keep_tail(t, tile, cols, tile * 2 + slot)
+                target = b_all if block < 2 else c_all
+                target[tile, slot] = made
             for g in range(2):
                 scores = lax.dot_general(
                     c_all[tile, g], b_all[tile, g], (((1,), (1,)), ((), ())), preferred_element_type=F32
@@ -318,70 +320,77 @@
             step = jnp.maximum(v, 0.0) + jnp.log1p(jnp.exp(-jnp.abs(v)))
             ld = jnp.dot(tri, -heads[1:2, :] * step, preferred_element_type=F32, precision=HIGHEST)
             last = ld[SEG - 1 : SEG, :]
-            ld_col[tile] = ld
-            ld_row[tile, :, 0:SEG] = ld.T
-            st_row[tile, :, 0:SEG] = step.T
-            e_ld[tile] = jnp.exp(ld).astype(BF16)
-            e_end[tile] = (jnp.exp(last - ld) * step).astype(BF16)
-            e_fin[tile] = jnp.broadcast_to(jnp.exp(last), (8, 128))
+            ld_col[tile] = ld * LOG2E
+            ld_row[tile, :, 0:SEG] = (ld * LOG2E - jnp.log2(step)).T
+            e_all[2 * tile * SEG : (2 * tile + 1) * SEG, :] = jnp.exp(ld).astype(BF16)
+            e_all[(2 * tile + 1) * SEG : (2 * tile + 2) * SEG, :] = (jnp.exp(last - ld) * step).astype(BF16)
+            e_fin[tile, 0:1, :] = jnp.exp(last)
+            e_fin[tile, 1:2, :] = heads[2:3, :]
+
+    low = lane < 64
 
     def step_of(t, q):
         g = lax.div(q, 4)
         base = c * 32 + q * 4
-        cols = pl.ds(mult(c * HALF + q * CHUNK, CHUNK), CHUNK)
+        first = lax.rem(128 - base, 128)
         proj[...] = dot(hg[...], w_main[q])
         spread = (
             lax.broadcasted_iota(jnp.int32, (128, CHUNK), 0)
             == base + lax.div(lax.broadcasted_iota(jnp.int32, (128, CHUNK), 1), 64)
         ).astype(F32)
-        spread16 = spread.astype(BF16)
-        weight, bias = conv_w[:, cols], conv_b[:, cols]
-        skip_now, gain_now = skip[:, cols], out_gain[:, cols]
+        spread_out[...] = dot(e_all[...], spread.astype(BF16))
         if t > 0:
             remote(s_recv.at[t - 1, q], s_recv.at[t - 1, q], st_send.at[t - 1, q], st_recv.at[t - 1, q], after).wait_recv()
         made = []
         for tile in range(2):
             rows = slice(tile * SEG, (tile + 1) * SEG)
             scale = rowscale[rows, :]
-            fresh = by_rows(proj[rows, 0:CHUNK], scale).astype(BF16).astype(F32)
-            x = conv(CHUNK, tail_of(t, tile, cols), fresh, weight, bias)
-            keep_tail(t, tile, cols, CHUNK)
+            half_scale = 0.5 * scale
             if t == 0:
                 state = s_in[tile, pl.ds(mult(q * CHUNK, CHUNK), CHUNK), :].T
             elif tile == 0:
                 state = jnp.where(m > 0, s_recv[t - 1, q].astype(F32), 0.0)
             else:
                 state = s_loc[q]
-            ld = pltpu.roll(ld_col[tile], lax.rem(128 - base, 128), 1)
+            ld = pltpu.roll(ld_col[tile], first, 1)
+            ends = pltpu.roll(e_fin[tile], first, 1)
             sa, sb = score_a[tile, g], score_b[tile, g]
-            pairs = []
+            carried = dot(c_all[tile, g], state.astype(BF16))
+            squares = jnp.zeros((SEG, 128), F32)
+            grown = []
             for pair in range(2):
-                xp = x[:, pair * 128 : pair * 128 + 128]
-                outs = []
-                for i in range(2):
-                    h = pair * 2 + i
+                lanes = slice(pair * 128, pair * 128 + 128)
+                cols = pl.ds(mult(c * HALF + q * CHUNK + pair * 128, 128), 128)
+                slot = tile * 2 + pair
+                x = conv(
+                    slot, tail_of(t, tile, cols), proj[rows, lanes] * scale, 0.5 * conv_w[:, cols], 0.5 * conv_b[:, cols]
+                )
+                keep_tail(t, tile, cols, slot)
+                weights = []
+                for h in (pair * 2, pair * 2 + 1):
                     col = jnp.broadcast_to(ld[:, h : h + 1], (SEG, 128))
                     ldr = ld_row[tile, pl.ds(base + h, 1), :]
-                    str_ = st_row[tile, pl.ds(base + h, 1), :]
-                    wa = sa * jnp.exp(jnp.minimum(col - ldr[:, 0:128], 0.0)) * str_[:, 0:128]
-                    wb = sb * jnp.exp(jnp.minimum(col[128:SEG, 0:32] - ldr[:, 128:SEG], 0.0)) * str_[:, 128:SEG]
-                    oa = dot(wa.astype(BF16), xp[0:128])
-                    ob = dot(wb.astype(BF16), xp[128:SEG])
-                    outs.append(jnp.concatenate([oa[0:128], oa[128:SEG] + ob], axis=0))
-                pairs.append(jnp.where(lane < 64, outs[0], outs[1]))
-            mixed = jnp.concatenate(pairs, axis=1)
-            carried = dot(c_all[tile, g], state.astype(BF16)) * dot(e_ld[tile], spread16)
-            wide = x.astype(F32)
-            combined = mixed + carried + skip_now * wide
-            out = combined * silu(by_rows(proj[rows, CHUNK : 2 * CHUNK], scale))
-            sq_mine[rows, :] += lane_sums(out * out)
-            gated[rows, pl.ds(mult(q * CHUNK, CHUNK), CHUNK)] = (out * gain_now).astype(BF16)
-            scaled = (wide * dot(e_end[tile], spread16)).astype(BF16)
-            grown = lax.dot_general(
-                b_all[tile, g], scaled, (((0,), (0,)), ((), ())), preferred_element_type=F32
-            )
-            fade = jnp.dot(e_fin[tile], spread, preferred_element_type=F32, precision=HIGHEST)
-            made.append(fade[0:1, :] * state + grown)
+                    wa = (sa * jnp.exp2(jnp.minimum(col - ldr[:, 0:128], 64.0))).astype(BF16)
+                    wb = (sb * jnp.exp2(jnp.minimum(col[128:SEG, 0:32] - ldr[:, 128:SEG], 64.0))).astype(BF16)
+                    wb = jnp.concatenate([jnp.zeros((128, 32), BF16), wb], axis=0)
+                    weights.append(jnp.concatenate([wa, wb], axis=1))
+                both = dot(jnp.concatenate(weights, axis=0), x)
+                mixed = jnp.where(low, both[0:SEG], both[SEG : 2 * SEG])
+                wide = x.astype(F32)
+                end = jnp.where(low[0:8], ends[:, 2 * pair : 2 * pair + 1], ends[:, 2 * pair + 1 : 2 * pair + 2])
+                e_now = spread_out[2 * tile * SEG : (2 * tile + 1) * SEG, lanes]
+                e_last = spread_out[(2 * tile + 1) * SEG : (2 * tile + 2) * SEG, lanes]
+                combined = mixed + carried[:, lanes] * e_now + end[1:2, :] * wide
+                gate = slice(CHUNK + pair * 128, CHUNK + pair * 128 + 128)
+                out = combined * silu_of_half(proj[rows, gate] * half_scale)
+                squares = squares + out * out
+                gated[rows, pl.ds(mult(q * CHUNK + pair * 128, 128), 128)] = (out * out_gain[:, cols]).astype(BF16)
+                grew = lax.dot_general(
+                    b_all[tile, g], (wide * e_last).astype(BF16), (((0,), (0,)), ((), ())), preferred_element_type=F32
+                )
+                grown.append(end[0:1, :] * state[:, lanes] + grew)
+            sq_mine[rows, :] += squares
+            made.append(jnp.concatenate(grown, axis=1))
         if t < 2:
             s_loc[q] = made[0]
             s_send[t, q] = made[1].astype(BF16)
@@ -481,14 +490,12 @@
 
         finish(t, PIECES - 1, rowscale[0:SEG, :])
 
-    for i, slot in enumerate(bc_slots):
-        sent(bc_landed()[i], 8, slot)
+    sent(bc_landed(), 8, 18)
     sent_x(bc_part, 8)
 
     @pl.loop(0, STEPS)
     def _(q):
-        for i, dst in enumerate(main_landed(q)):
-            sent(dst, q, 18 + i)
+        sent(main_landed(q), q, 18)
         sent_x(functools.partial(x_part, q), q)
         sent_g(functools.partial(g_part, q), q)
         place = state_out.at[pl.ds(mult(c * HALF + q * CHUNK, CHUNK), CHUNK), :]
@@ -516,18 +523,32 @@
             remote(part, part, r_send.at[t, n], r_recv.at[t, n], sib).wait_send()
 
 
+def hand_over(panel, state, panel_out, state_out, panel_here, state_here, sem_in, sem_out):
+    pieces = [(panel, panel_here, panel_out)]
+    for i in range(4):
+        rows = pl.ds(i * 1024, 1024)
+        pieces.append((state.at[rows, :], state_here.at[rows, :], state_out.at[rows, :]))
+    for i, (src, here, _) in enumerate(pieces):
+        pltpu.make_async_copy(src, here, sem_in.at[i]).start()
+    for i, (src, here, dst) in enumerate(pieces):
+        pltpu.make_async_copy(src, here, sem_in.at[i]).wait()
+        pltpu.make_async_copy(here, dst, sem_out.at[i]).start()
+    for i, (_, here, dst) in enumerate(pieces):
+        pltpu.make_async_copy(here, dst, sem_out.at[i]).wait()
+
+
 def local(
     panels, feed, ssm_state, conv_state, w_in, w_out, norm_gain, conv_weight, conv_bias,
     dt_bias, decay_rate, skip_gain, out_gain,
 ):
-    tail = jnp.pad(conv_state[0, 0].astype(F32), ((5, 0), (0, 0)))
-    w_dt = jnp.pad(w_in[0, :, 9216:], ((0, 0), (0, 64)))
-    heads = jnp.pad(jnp.concatenate([dt_bias, decay_rate], axis=0), ((0, 6), (0, 64)))
-    skip = jnp.repeat(skip_gain, 64, axis=1)
     any_ = pl.BlockSpec(memory_space=pl.ANY)
     vmem = pl.BlockSpec(memory_space=pltpu.VMEM)
     dma = pltpu.SemaphoreType.DMA
     scratch = [
+        pltpu.VMEM((9280, 128), BF16),
+        pltpu.VMEM((STEPS, 128, 512), BF16),
+        pltpu.VMEM((128, 640), BF16),
+        pltpu.VMEM((8, 128), F32),
         pltpu.VMEM((STEPS, 2048, 512), BF16),
         pltpu.VMEM((2048, 640), BF16),
         pltpu.VMEM((HALF, WIDTH), BF16),
@@ -542,17 +563,16 @@
         pltpu.VMEM((2, STEPS, 128, CHUNK), BF16),
         pltpu.VMEM((2, STEPS, CHUNK, 128), F32),
         pltpu.VMEM((2, SEG, WIDTH), BF16),
-        pltpu.VMEM((SEG + 8, 256), F32),
+        pltpu.VMEM((4, SEG + 8, 128), F32),
         pltpu.VMEM((2 * SEG, 512), F32),
+        pltpu.VMEM((4 * SEG, CHUNK), F32),
         pltpu.VMEM((2, 2, SEG, 128), BF16),
         pltpu.VMEM((2, 2, SEG, 128), BF16),
         pltpu.VMEM((2, 2, SEG, 128), F32),
         pltpu.VMEM((2, 2, 32, 32), F32),
         pltpu.VMEM((2, SEG, 128), F32),
         pltpu.VMEM((2, 128, 256), F32),
-        pltpu.VMEM((2, 128, 256), F32),
-        pltpu.VMEM((2, SEG, 128), BF16),
-        pltpu.VMEM((2, SEG, 128), BF16),
+        pltpu.VMEM((4 * SEG, 128), BF16),
         pltpu.VMEM((2, 8, 128), F32),
         pltpu.VMEM((2 * SEG, HALF), BF16),
         pltpu.VMEM((PIECES, SEG, PIECE), F32),
@@ -562,7 +582,7 @@
         pltpu.VMEM((3, SEG, 128), F32),
         pltpu.VMEM((3, SEG, 128), F32),
         pltpu.VMEM((2, SEG, WIDTH), BF16),
-        dma((9, 20)), dma((9, 20)), dma((9, 3)), dma((5,)), dma((8,)), dma((8,)),
+        dma((9, 19)), dma((9, 19)), dma((7,)), dma((8,)), dma((8,)),
         dma((3, PIECES)), dma((3, PIECES)), dma((2, PIECES)), dma((2, PIECES)), dma((2, PIECES)), dma((2, PIECES)),
         dma((2, STEPS)), dma((2, STEPS)), dma((STEPS,)), dma((STEPS,)), dma((STEPS,)),
     ]
@@ -572,7 +592,7 @@
             jax.ShapeDtypeStruct((SEG, WIDTH), BF16),
             jax.ShapeDtypeStruct((4096, 128), F32),
         ),
-        in_specs=[any_, any_, any_, any_, any_, any_, any_] + [vmem] * 6,
+        in_specs=[any_] * 5 + [vmem] * 8,
         out_specs=(vmem, any_),
         scratch_shapes=scratch,
         compiler_params=pltpu.CompilerParams(
@@ -580,9 +600,17 @@
         ),
         cost_estimate=pl.CostEstimate(flops=28_000_000_000, bytes_accessed=60_000_000, transcendentals=20_000_000),
     )(
-        panels[0], feed, ssm_state.reshape(4096, 128), tail, w_in[0], w_dt, w_out[0],
-        norm_gain, conv_weight[0], conv_bias, heads, skip, out_gain,
+        panels[0], feed, ssm_state.reshape(4096, 128), w_in[0].T, w_out[0], conv_state[0, 0],
+        norm_gain, conv_weight[0], conv_bias, dt_bias, decay_rate, skip_gain, out_gain,
     )
+    panel, state = pl.pallas_call(
+        hand_over,
+        out_shape=(jax.ShapeDtypeStruct((SEG, WIDTH), BF16), jax.ShapeDtypeStruct((4096, 128), F32)),
+        in_specs=[any_, any_],
+        out_specs=(any_, any_),
+        scratch_shapes=[pltpu.VMEM((SEG, WIDTH), BF16), pltpu.VMEM((4096, 128), F32), dma((5,)), dma((5,))],
+        compiler_params=pltpu.CompilerParams(vmem_limit_bytes=60 * 1024 * 1024),
+    )(panel, state)
     return (panel[None], state.reshape(1, 1, 64, 64, 128))
 
 

time: 251 us -> 237 us (0.944)
  local copies, waits for them, and re-layouts: 11.1 us -> 0 us
  other arithmetic: 2.75 us -> 0 us
    unnamed x5 -> x0, local copies, waits for them, and re-layouts: 9 us -> none
    pallas_call x0 -> x1, Pallas kernels: none -> 2.7 us  [local(): pl.pallas_call(hand_over, out_shape=(jax.ShapeDtypeStruct((SEG, WIDTH), B...]
    pallas_call x1, Pallas kernels: 235 us -> 232 us  [local(): pl.pallas_call(kernel, out_shape=(jax.ShapeDtypeStruct((SEG, WIDTH), BF16...]
where the time goes in v2:
time: 237 us; the launch traced here: 236 us
  Pallas kernels  235 us (99%)
    pallas_call x1, Pallas kernels, local(): pl.pallas_call(kernel, out_shape=(jax.ShapeDtypeStruct((SEG, WIDTH), BF16...  232 us

profile of v2, /device:TPU:2, one launch (start us, length us, event | category | flops | bytes accessed | tf_op | source)
XLA Modules:
  0.0 235.6 jit_solution(3536718537816683367)
XLA Ops:
  0.6 232.1 %shard_map.140 = (bf16[160,2048]{1,0:T(8,128)(2,1)}, f32[4096,128]{1,0:T(8,128)}) custom-call(bf16[160,2048]{1,0:T(8,128)(2,1)} %bitcast.14, bf16[2,160,2048]{2,1,0:T(8,128)(2,1)} %feed.1, f32[4096,128]{1,0:T(8,128)} %bitcast.12, bf16[9280,128]{1,0:T(8,128)(2,1)} %bitcast.11, bf16[4096,2048]{1,0:T(8,128)(2,1)} %bitcast.10, bf16[3,5120]{1,0:T(4,128)(2,1)} %bitcast.17, ...), custom_call_target="tpu_custom_call" | custom-call | flops 28000000000 | bytes 60000000 | tf_op jit(solution)/shard_map/pallas_call | solution.py:589
  232.7 2.7 %shard_map.141 = (bf16[160,2048]{1,0:T(8,128)(2,1)}, f32[4096,128]{1,0:T(8,128)}) custom-call(bf16[160,2048]{1,0:T(8,128)(2,1)} %get-tuple-element.6.panel, f32[4096,128]{1,0:T(8,128)} %get-tuple-element.7.state), custom_call_target="tpu_custom_call" | custom-call | tf_op jit(solution)/shard_map/pallas_call | solution.py:606

commit v3 on v2

v3 whole, which is shorter than its diff:
```python
import functools

import jax
import jax.numpy as jnp
from jax import lax
from jax.experimental import pallas as pl
from jax.experimental.pallas import tpu as pltpu
from jax.sharding import PartitionSpec as P

EPS = 1e-05
LOG2E = 1.4426950408889634
F32 = jnp.float32
BF16 = jnp.bfloat16
SEG = 160
WIDTH = 2048
HALF = 2048
CHUNK = 256
STEPS = HALF // CHUNK
PIECE = 512
PIECES = WIDTH // PIECE
MESH = pl.DeviceIdType.MESH


def silu_of_half(half):
    return half + half * jnp.tanh(half)


def dot(a, b):
    return jnp.dot(a, b, preferred_element_type=F32)


def by_rows(v, scale):
    blocks = [v[:, i : i + 128] * scale for i in range(0, v.shape[1], 128)]
    return blocks[0] if len(blocks) == 1 else jnp.concatenate(blocks, axis=1)


def lane_sums(v):
    total = v[:, :128]
    for i in range(128, v.shape[1], 128):
        total = total + v[:, i : i + 128]
    return total


def kernel(
    panels, feed, state_in, w_in, w_out, tail_in, norm_gain, conv_w, conv_b, dt_bias, decay_rate, skip_gain, out_gain,
    panel_out, state_out,
    w_rows, w_cut, bc_cut, heads,
    w_main, w_bc, w_o, hid, hg, ssq, rowscale, tails, x_loc, bc_loc, bc_to, bc_from, s_in, s_loc, s_send, s_recv, fd,
    convbuf, proj, made_a, made_b, b_all, c_all, score_a, score_b, ld_col, ld_row, e_all, e_fin,
    gated, own_part, part_send, part_recv, sq_mine, sq_send, sq_recv, pan_send, pan_stage,
    g_send, g_recv, l_sem, m_send, m_recv, p_send, p_recv, n_send, n_recv, r_send, r_recv,
    st_send, st_recv, f_send, f_recv, f_loc, q_send, q_recv, o_send, o_recv, o_loc,
):
    layer = lax.axis_index("layer")
    seq = lax.axis_index("seq")
    c = lax.rem(seq, 2)
    m = lax.div(seq, 2)
    y = lax.rem(m, 4)
    z = lax.div(m, 4)
    oc = 1 - c
    yp = lax.rem(y + 1, 4)
    ym = lax.rem(y + 3, 4)
    y2 = lax.rem(y + 2, 4)
    oz = 1 - z

    def at(zz, yy, cc):
        return (layer, zz * 8 + yy * 2 + cc)

    sib = at(z, y, oc)
    to_yp = at(z, yp, c)
    to_ym = at(z, ym, c)
    to_z = at(oz, y, c)
    up = (lax.rem(layer + 1, 8), seq)
    down = (lax.rem(layer + 7, 8), seq)
    after = (layer, lax.rem(seq + 2, 16))
    before = (layer, lax.rem(seq + 14, 16))

    def mult(v, by):
        return pl.multiple_of(v, by)

    local = (
        (w_in.at[pl.ds(8192, 1088), :], w_rows.at[pl.ds(8192, 1088), :]),
        (w_in.at[pl.ds(4096, 4096), :], w_rows.at[pl.ds(4096, 4096), :]),
        (w_in.at[pl.ds(0, 4096), :], w_rows.at[pl.ds(0, 4096), :]),
        (panels, hid.at[0, c]),
        (state_in.at[pl.ds(mult(c * HALF, HALF), HALF), :], s_in.at[c]),
        (w_out.at[pl.ds(mult(c * HALF, HALF), HALF), :], w_o),
        (feed.at[:, :, pl.ds(mult(c * 1024, 1024), 1024)], fd.at[:, c]),
    )
    for i, (src, dst) in enumerate(local[:3]):
        pltpu.make_async_copy(src, dst, l_sem.at[i]).start()

    barrier = pltpu.get_barrier_semaphore()
    friends = (sib, to_yp, to_ym, to_z, up, down, after, before)
    for friend in friends:
        pl.semaphore_signal(barrier, inc=1, device_id=friend, device_id_type=MESH)

    heads[...] = jnp.zeros((8, 128), F32)
    heads[0:1, 0:64] = dt_bias[...]
    heads[1:2, 0:64] = decay_rate[...]
    heads[2:3, 0:64] = skip_gain[...]
    tails[c, 0:8, :] = jnp.zeros((8, 5120), F32)
    tails[c, 5:8, :] = tail_in[...].astype(F32)

    for i, (src, dst) in enumerate(local[:3]):
        pltpu.make_async_copy(src, dst, l_sem.at[i]).wait()
    pl.semaphore_wait(barrier, len(friends))

    def remote(src, dst, ss, rs, who):
        return pltpu.make_async_remote_copy(
            src_ref=src, dst_ref=dst, send_sem=ss, recv_sem=rs, device_id=who, device_id_type=MESH
        )

    own_rows = mult(m * 256 + c * 128, 128)
    sib_rows = mult(m * 256 + oc * 128, 128)

    def turned(start, size):
        return w_rows[pl.ds(mult(start, 64), size), :].T

    def bc_prepare():
        dt = jnp.concatenate([turned(9216, 64), jnp.zeros((128, 64), BF16)], axis=1)
        rows = pl.ds(own_rows, 128)
        for cc, target, where in ((c, w_bc, rows), (oc, bc_cut, slice(0, 128))):
            target[where, 0:256] = turned(8192 + cc * 256, 256)
            target[where, 256:512] = turned(8704 + cc * 256, 256)
            target[where, 512:640] = dt
        remote(bc_cut, w_bc.at[rows, :], g_send.at[8, 18], g_recv.at[8, 18], sib).start()

    def main_prepare(q):
        rows = pl.ds(own_rows, 128)
        w_main[q, rows, 0:256] = turned(4096 + c * 2048 + q * 256, 256)
        w_main[q, rows, 256:512] = turned(c * 2048 + q * 256, 256)
        w_cut[q, :, 0:256] = turned(4096 + oc * 2048 + q * 256, 256)
        w_cut[q, :, 256:512] = turned(oc * 2048 + q * 256, 256)
        remote(w_cut.at[q], w_main.at[q, rows, :], g_send.at[q, 18], g_recv.at[q, 18], sib).start()

    def bc_landed():
        return w_bc.at[pl.ds(sib_rows, 128), :]

    def main_landed(q):
        return w_main.at[q, pl.ds(sib_rows, 128), :]

    def bc_part(mm, half=None):
        if half is None:
            return w_bc.at[pl.ds(mult(mm * 256, 256), 256), :]
        return w_bc.at[pl.ds(mult(mm * 256 + half * 128, 128), 128), :]

    def main_part(q, mm, half=None):
        if half is None:
            return w_main.at[q, pl.ds(mult(mm * 256, 256), 256), :]
        return w_main.at[q, pl.ds(mult(mm * 256 + half * 128, 128), 128), :]

    def part_of(q):
        return functools.partial(main_part, q)

    m_yp, m_ym, m_y2 = z * 4 + yp, z * 4 + ym, z * 4 + y2
    o_y, o_yp, o_ym, o_y2 = oz * 4 + y, oz * 4 + yp, oz * 4 + ym, oz * 4 + y2

    def push(part, q, slot, who):
        remote(part, part, g_send.at[q, slot], g_recv.at[q, slot], who).start()

    def arrived(part, q, slot):
        remote(part, part, g_send.at[q, slot], g_recv.at[q, slot], sib).wait_recv()

    def sent(part, q, slot):
        remote(part, part, g_send.at[q, slot], g_recv.at[q, slot], sib).wait_send()

    def first_x(part, q):
        push(part(m), q, 2, to_z)
        push(part(m), q, 0, to_yp)
        push(part(m), q, 1, to_ym)

    def first_g(part, q):
        push(part(m), q, 5, to_z)
        push(part(m), q, 3, to_yp)
        push(part(m), q, 4, to_ym)

    def second_x(part, q):
        arrived(part(o_y), q, 2)
        push(part(o_y), q, 6, to_yp)
        push(part(o_y), q, 7, to_ym)
        arrived(part(m_ym), q, 0)
        push(part(m_ym, 0), q, 8, to_yp)
        arrived(part(m_yp), q, 1)
        push(part(m_yp, 1), q, 9, to_ym)

    def second_g(part, q):
        arrived(part(m_ym), q, 3)
        push(part(m_ym), q, 11, to_z)
        push(part(m_ym, 0), q, 10, to_yp)
        arrived(part(m_yp), q, 4)
        push(part(m_yp), q, 13, to_z)
        push(part(m_yp, 1), q, 12, to_ym)
        arrived(part(o_y), q, 5)

    def third_x(part, q):
        arrived(part(o_ym), q, 6)
        push(part(o_ym, 0), q, 14, to_yp)
        arrived(part(o_yp), q, 7)
        push(part(o_yp, 1), q, 15, to_ym)
        arrived(part(m_y2, 0), q, 8)
        arrived(part(m_y2, 1), q, 9)

    def third_g(part, q):
        arrived(part(m_y2, 0), q, 10)
        push(part(m_y2, 0), q, 16, to_z)
        arrived(part(m_y2, 1), q, 12)
        push(part(m_y2, 1), q, 17, to_z)
        arrived(part(o_ym), q, 11)
        arrived(part(o_yp), q, 13)

    def last_x(part, q):
        arrived(part(o_y2, 0), q, 14)
        arrived(part(o_y2, 1), q, 15)

    def last_g(part, q):
        arrived(part(o_y2, 0), q, 16)
        arrived(part(o_y2, 1), q, 17)

    def sent_x(part, q):
        for slot in (0, 1, 2, 6, 7):
            sent(part(m), q, slot)
        for slot in (8, 9, 14, 15):
            sent(part(m, 0), q, slot)

    def sent_g(part, q):
        for slot in (3, 4, 5, 11, 13):
            sent(part(m), q, slot)
        for slot in (10, 12, 16, 17):
            sent(part(m, 0), q, slot)

    bc_prepare()
    main_prepare(0)
    arrived(bc_landed(), 8, 18)
    first_x(bc_part, 8)

    @pl.loop(0, STEPS // 2)
    def _(i):
        q = 2 * i
        main_prepare(q + 1)
        arrived(main_landed(q), q, 18)
        first_x(part_of(q), q)

        @pl.when(i < STEPS // 2 - 1)
        def _():
            main_prepare(q + 2)

        arrived(main_landed(q + 1), q + 1, 18)
        first_g(part_of(q + 1), q + 1)

    begin = (
        (panels, hid.at[0, c], 0),
        (tails.at[c], tails.at[c], 1),
        (state_in.at[pl.ds(mult(oc * HALF, HALF), HALF), :], s_in.at[c], 2),
        (feed.at[:, :, pl.ds(mult(oc * 1024, 1024), 1024)], fd.at[:, c], 3),
    )
    for src, dst, i in begin:
        remote(src, dst, m_send.at[i], m_recv.at[i], sib).start()
    for i, (src, dst) in enumerate(local[3:]):
        pltpu.make_async_copy(src, dst, l_sem.at[3 + i]).start()
    for i, (src, dst) in enumerate(local[3:]):
        pltpu.make_async_copy(src, dst, l_sem.at[3 + i]).wait()
    for (src, dst, i), land in zip(begin, (hid.at[0, oc], tails.at[oc], s_in.at[oc], fd.at[:, oc])):
        remote(land, land, m_send.at[i], m_recv.at[i], sib).wait_recv()

    def ingest(t, tile, n):
        cols = pl.ds(mult(n * PIECE, PIECE), PIECE)
        rows = pl.ds(mult(tile * SEG, 32), SEG)
        h = hid[t, tile, :, cols].astype(F32)
        ssq[rows, :] += lane_sums(h * h)
        hg[rows, cols] = (h * norm_gain[:, cols]).astype(BF16)

    lane = lax.broadcasted_iota(jnp.int32, (SEG, 128), 1)
    row = lax.broadcasted_iota(jnp.int32, (SEG, 128), 0)

    def conv(slot, tile_tail, fresh, weight, bias):
        convbuf[slot, 0:8, :] = tile_tail
        convbuf[slot, 8 : 8 + SEG, :] = fresh
        total = bias
        for k in range(4):
            total = total + convbuf[slot, 5 + k : 5 + k + SEG, :] * weight[k : k + 1, :]
        return silu_of_half(total).astype(BF16)

    def x_tail(t, tile, q, pair, cols):
        lanes = slice(pair * 128, pair * 128 + 128)
        if t == 0:
            return tails[tile, :, cols]
        if tile == 1:
            return x_loc[t - 1, q, :, lanes]
        return jnp.where(m > 0, s_recv[t - 1, q, 128:144, lanes].astype(F32)[8:16], 0.0)

    def bc_tail(t, tile, block, cols):
        lanes = slice(block * 128, block * 128 + 128)
        if t == 0:
            return tails[tile, :, cols]
        if tile == 1:
            return bc_loc[t - 1, :, lanes]
        return jnp.where(m > 0, bc_from[t - 1, :, lanes].astype(F32)[8:16], 0.0)

    def keep_tail(t, tile, slot, here, away):
        if t < 2 and tile == 0:
            target, at_ = here
            target[at_] = convbuf[slot, SEG : SEG + 8, :]
        elif t < 2:
            target, at_ = away
            target[at_] = convbuf[slot, SEG - 8 : SEG + 8, :].astype(BF16)

    def prologue(t, tile):
        rows = slice(tile * SEG, (tile + 1) * SEG)
        if t > 0 and tile == 0:
            remote(bc_to.at[t - 1], bc_from.at[t - 1], m_send.at[3 + t], m_recv.at[3 + t], after).wait_recv()
        total = jnp.sum(ssq[rows, :], axis=1, keepdims=True)
        rowscale[rows, :] = jnp.broadcast_to(lax.rsqrt(total * (1.0 / WIDTH) + EPS), (SEG, 128))
        proj[...] = dot(hg[rows, :], w_bc[...])
        causal = lane <= row
        tri = (
            lax.broadcasted_iota(jnp.int32, (SEG, SEG), 1) <= lax.broadcasted_iota(jnp.int32, (SEG, SEG), 0)
        ).astype(BF16)
        sq_mine[rows, :] = jnp.zeros((SEG, 128), F32)
        scale = rowscale[rows, :]
        for block in range(4):
            slot = block % 2
            base = 4096 if block < 2 else 4608
            cols = pl.ds(mult(base + c * 256 + slot * 128, 128), 128)
            fresh = proj[:, block * 128 : block * 128 + 128] * scale
            made = conv(
                tile * 2 + slot, bc_tail(t, tile, block, cols), fresh, 0.5 * conv_w[:, cols], 0.5 * conv_b[:, cols]
            )
            lanes = slice(block * 128, block * 128 + 128)
            keep_tail(t, tile, tile * 2 + slot, (bc_loc, (min(t, 1), slice(0, 8), lanes)), (bc_to, (min(t, 1), slice(0, 16), lanes)))
            target = b_all if block < 2 else c_all
            target[tile, slot] = made
        for g in range(2):
            scores = lax.dot_general(
                c_all[tile, g], b_all[tile, g], (((1,), (1,)), ((), ())), preferred_element_type=F32
            )
            score_a[tile, g] = jnp.where(causal, scores[:, 0:128], 0.0)
            score_b[tile, g] = jnp.where(causal[0:32, 0:32], scores[128:SEG, 128:SEG], 0.0)
        v = proj[:, 512:640] * scale + heads[0:1, :]
        step = jnp.maximum(v, 0.0) + jnp.log1p(jnp.exp(-jnp.abs(v)))
        fall = -heads[1:2, :] * step
        coarse = fall.astype(BF16)
        rest = fall - coarse.astype(F32)
        fine = rest.astype(BF16)
        finest = (rest - fine.astype(F32)).astype(BF16)
        sums = dot(tri, jnp.concatenate([coarse, fine, finest], axis=1))
        ld = sums[:, 0:128] + (sums[:, 128:256] + sums[:, 256:384])
        last = ld[SEG - 1 : SEG, :]
        ld_col[tile] = ld * LOG2E
        ld_row[tile, :, 0:SEG] = (ld * LOG2E - jnp.log2(step)).T
        e_all[2 * tile * SEG : (2 * tile + 1) * SEG, :] = jnp.exp(ld).astype(BF16)
        e_all[(2 * tile + 1) * SEG : (2 * tile + 2) * SEG, :] = (jnp.exp(last - ld) * step).astype(BF16)
        e_fin[tile, 0:1, :] = jnp.exp(last)
        e_fin[tile, 1:2, :] = heads[2:3, :]

        if t < 2 and tile == 1:
            remote(bc_to.at[t], bc_from.at[t], m_send.at[4 + t], m_recv.at[4 + t], after).start()

    low = lane < 64

    def project(tile, q, into):
        into[...] = dot(hg[tile * SEG : (tile + 1) * SEG, :], w_main[q])

    def state_arrived(t, q):
        land = s_recv.at[t - 1, q]
        remote(land, land, st_send.at[t - 1, q], st_recv.at[t - 1, q], after).wait_recv()

    def step_of(t, tile, q, made_of):
        rows = slice(tile * SEG, (tile + 1) * SEG)
        g = lax.div(q, 4)
        base = c * 32 + q * 4
        first = lax.rem(128 - base, 128)
        spread = (
            lax.broadcasted_iota(jnp.int32, (128, CHUNK), 0)
            == base + lax.div(lax.broadcasted_iota(jnp.int32, (128, CHUNK), 1), 64)
        ).astype(F32)
        both_e = slice(2 * tile * SEG, (2 * tile + 2) * SEG)
        spread_out = dot(e_all[both_e, :], spread.astype(BF16))
        scale = rowscale[rows, :]
        half_scale = 0.5 * scale
        if t == 0:
            state = s_in[tile, pl.ds(mult(q * CHUNK, CHUNK), CHUNK), :].T
        elif tile == 0:
            state = jnp.where(m > 0, s_recv[t - 1, q, 0:128, :].astype(F32), 0.0)
        else:
            state = s_loc[t - 1, q]
        ld = pltpu.roll(ld_col[tile], first, 1)
        ends = pltpu.roll(e_fin[tile], first, 1)
        sa, sb = score_a[tile, g], score_b[tile, g]
        carried = dot(c_all[tile, g], state.astype(BF16))
        squares = jnp.zeros((SEG, 128), F32)
        grown = []
        for pair in range(2):
            lanes = slice(pair * 128, pair * 128 + 128)
            cols = pl.ds(mult(c * HALF + q * CHUNK + pair * 128, 128), 128)
            slot = tile * 2 + pair
            x = conv(
                slot, x_tail(t, tile, q, pair, cols), made_of[:, lanes] * scale, 0.5 * conv_w[:, cols], 0.5 * conv_b[:, cols]
            )
            keep_tail(t, tile, slot, (x_loc, (min(t, 1), q, slice(0, 8), lanes)), (s_send, (min(t, 1), q, slice(128, 144), lanes)))
            weights = []
            for h in (pair * 2, pair * 2 + 1):
                col = jnp.broadcast_to(ld[:, h : h + 1], (SEG, 128))
                ldr = ld_row[tile, pl.ds(base + h, 1), :]
                wa = (sa * jnp.exp2(jnp.minimum(col - ldr[:, 0:128], 64.0))).astype(BF16)
                wb = (sb * jnp.exp2(jnp.minimum(col[128:SEG, 0:32] - ldr[:, 128:SEG], 64.0))).astype(BF16)
                wb = jnp.concatenate([jnp.zeros((128, 32), BF16), wb], axis=0)
                weights.append(jnp.concatenate([wa, wb], axis=1))
            both = dot(jnp.concatenate(weights, axis=0), x)
            mixed = jnp.where(low, both[0:SEG], both[SEG : 2 * SEG])
            wide = x.astype(F32)
            end = jnp.where(low[0:8], ends[:, 2 * pair : 2 * pair + 1], ends[:, 2 * pair + 1 : 2 * pair + 2])
            e_now = spread_out[0:SEG, lanes]
            e_last = spread_out[SEG : 2 * SEG, lanes]
            combined = mixed + carried[:, lanes] * e_now + end[1:2, :] * wide
            gate = slice(CHUNK + pair * 128, CHUNK + pair * 128 + 128)
            out = combined * silu_of_half(made_of[:, gate] * half_scale)
            squares = squares + out * out
            gated[rows, pl.ds(mult(q * CHUNK + pair * 128, 128), 128)] = (out * out_gain[:, cols]).astype(BF16)
            grew = lax.dot_general(
                b_all[tile, g], (wide * e_last).astype(BF16), (((0,), (0,)), ((), ())), preferred_element_type=F32
            )
            grown.append(end[0:1, :] * state[:, lanes] + grew)
        sq_mine[rows, :] += squares
        made = jnp.concatenate(grown, axis=1)
        if t < 2 and tile == 0:
            s_loc[t, q] = made
        elif t < 2:
            s_send[t, q, 0:128, :] = made.astype(BF16)
        else:
            s_in[tile, pl.ds(mult(q * CHUNK, CHUNK), CHUNK), :] = made.T

    def state_off(t, tile, q):
        if t < 2 and tile == 1:
            remote(s_send.at[t, q], s_recv.at[t, q], st_send.at[t, q], st_recv.at[t, q], after).start()
        elif t == 2:
            place = state_out.at[pl.ds(mult(c * HALF + q * CHUNK, CHUNK), CHUNK), :]
            turned_q = pl.ds(mult(q * CHUNK, CHUNK), CHUNK)

            @pl.when(c == tile)
            def _():
                pltpu.make_async_copy(s_in.at[tile, turned_q, :], place, f_loc.at[q]).start()

            @pl.when(c != tile)
            def _():
                remote(s_in.at[tile, turned_q, :], place, f_send.at[q], f_recv.at[q], sib).start()

    def piece_cols(half, p):
        return pl.ds(mult(half * 1024 + p * PIECE, PIECE), PIECE)

    def emit(t, tile):
        rows = slice(tile * SEG, (tile + 1) * SEG)
        sq_send[t, tile] = sq_mine[rows, :]
        remote(sq_send.at[t, tile], sq_recv.at[t, tile], q_send.at[t, tile], q_recv.at[t, tile], sib).start()

        @pl.loop(0, 2)
        def _(p):
            part_send[t, tile, p] = dot(gated[rows, :], w_o[:, piece_cols(oc, p)]).astype(BF16)
            remote(
                part_send.at[t, tile, p], part_recv.at[t, tile, p], p_send.at[t, tile, p], p_recv.at[t, tile, p], sib
            ).start()

        @pl.loop(0, 2)
        def _(p):
            own_part[p] = dot(gated[rows, :], w_o[:, piece_cols(c, p)])

        if (t, tile) == (1, 0):
            relay(1, 1)
        remote(sq_recv.at[t, tile], sq_recv.at[t, tile], q_send.at[t, tile], q_recv.at[t, tile], sib).wait_recv()
        squares = jnp.sum(sq_mine[rows, :] + sq_recv[t, tile], axis=1, keepdims=True)
        scale = jnp.broadcast_to(lax.rsqrt(squares * (1.0 / 4096) + EPS), (SEG, 128))
        for p in range(2):
            land = part_recv.at[t, tile, p]
            remote(land, land, p_send.at[t, tile, p], p_recv.at[t, tile, p], sib).wait_recv()
            whole = own_part[p] + part_recv[t, tile, p].astype(F32)
            cols = piece_cols(c, p)
            panel = hid[t, tile, :, cols].astype(F32) + by_rows(whole, scale)
            if t < 2:
                entering = fd[t, tile, :, p * PIECE : (p + 1) * PIECE].astype(F32)
                pan_send[t, tile, p] = jnp.where(layer == 7, entering, panel).astype(BF16)
                remote(
                    pan_send.at[t, tile, p], hid.at[t + 1, tile, :, cols], n_send.at[t, tile, p], n_recv.at[t, tile, p], up
                ).start()
            else:
                pan_stage[tile, p] = panel.astype(BF16)

                @pl.when(c == tile)
                def _():
                    pltpu.make_async_copy(pan_stage.at[tile, p], panel_out.at[:, cols], o_loc.at[p]).start()

                @pl.when(c != tile)
                def _():
                    remote(pan_stage.at[tile, p], panel_out.at[:, cols], o_send.at[p], o_recv.at[p], sib).start()

    def relay(t, tile):
        for p in range(2):
            part = hid.at[t, tile, :, piece_cols(c, p)]
            remote(part, part, n_send.at[t - 1, tile, p], n_recv.at[t - 1, tile, p], up).wait_recv()
            remote(part, part, r_send.at[t - 1, tile, p], r_recv.at[t - 1, tile, p], sib).start()

    def receive(t, tile):
        for p in range(2):
            ingest(t, tile, c * 2 + p)
        for p in range(2):
            part = hid.at[t, tile, :, piece_cols(oc, p)]
            remote(part, part, r_send.at[t - 1, tile, p], r_recv.at[t - 1, tile, p], sib).wait_recv()
            ingest(t, tile, oc * 2 + p)

    ssq[...] = jnp.zeros((2 * SEG, 128), F32)

    @pl.loop(0, 2 * PIECES)
    def _(i):
        ingest(0, lax.rem(i, 2), lax.div(i, 2))

    second_x(bc_part, 8)

    @pl.loop(0, STEPS // 2)
    def _(i):
        second_x(part_of(2 * i), 2 * i)
        second_g(part_of(2 * i + 1), 2 * i + 1)

    third_x(bc_part, 8)

    @pl.loop(0, STEPS // 2)
    def _(i):
        third_x(part_of(2 * i), 2 * i)
        third_g(part_of(2 * i + 1), 2 * i + 1)

    last_x(bc_part, 8)
    for tile in range(2):
        prologue(0, tile)

    @pl.loop(0, STEPS)
    def _(q):
        @pl.when(lax.rem(q, 2) == 0)
        def _():
            last_x(part_of(q), q)

        @pl.when(lax.rem(q, 2) == 1)
        def _():
            last_g(part_of(q), q)

        project(0, q, made_a)
        project(1, q, made_b)
        step_of(0, 0, q, made_a)
        step_of(0, 1, q, made_b)
        state_off(0, 1, q)

    for tile in range(2):
        emit(0, tile)

    for t in (1, 2):
        for tile in range(2):
            ssq[tile * SEG : (tile + 1) * SEG, :] = jnp.zeros((SEG, 128), F32)
            if (t, tile) != (1, 1):
                relay(t, tile)
            receive(t, tile)
            prologue(t, tile)

            project(tile, 0, made_a)

            @pl.loop(0, STEPS // 2)
            def _(i):
                q = 2 * i
                if tile == 0:
                    state_arrived(t, q)
                    state_arrived(t, q + 1)
                project(tile, q + 1, made_b)
                step_of(t, tile, q, made_a)
                project(tile, lax.rem(q + 2, STEPS), made_a)
                step_of(t, tile, q + 1, made_b)
                state_off(t, tile, q)
                state_off(t, tile, q + 1)

            emit(t, tile)

    sent(bc_landed(), 8, 18)
    sent_x(bc_part, 8)

    @pl.loop(0, STEPS)
    def _(q):
        sent(main_landed(q), q, 18)

        @pl.when(lax.rem(q, 2) == 0)
        def _():
            sent_x(part_of(q), q)

        @pl.when(lax.rem(q, 2) == 1)
        def _():
            sent_g(part_of(q), q)

        place = state_out.at[pl.ds(mult(c * HALF + q * CHUNK, CHUNK), CHUNK), :]
        land = state_out.at[pl.ds(mult(oc * HALF + q * CHUNK, CHUNK), CHUNK), :]
        turned_q = pl.ds(mult(q * CHUNK, CHUNK), CHUNK)
        pltpu.make_async_copy(s_in.at[c, turned_q, :], place, f_loc.at[q]).wait()
        remote(s_in.at[oc, turned_q, :], land, f_send.at[q], f_recv.at[q], sib).wait()
        for t in range(2):
            remote(s_send.at[t, q], s_recv.at[t, q], st_send.at[t, q], st_recv.at[t, q], after).wait_send()

    for src, dst, i in begin:
        remote(src, dst, m_send.at[i], m_recv.at[i], sib).wait_send()
    for t in range(2):
        remote(bc_to.at[t], bc_from.at[t], m_send.at[4 + t], m_recv.at[4 + t], after).wait_send()

    for p in range(2):
        pltpu.make_async_copy(pan_stage.at[c, p], panel_out.at[:, piece_cols(c, p)], o_loc.at[p]).wait()
        remote(pan_stage.at[oc, p], panel_out.at[:, piece_cols(oc, p)], o_send.at[p], o_recv.at[p], sib).wait()

    @pl.loop(0, 2)
    def _(tile):
        for t in range(3):
            remote(sq_send.at[t, tile], sq_recv.at[t, tile], q_send.at[t, tile], q_recv.at[t, tile], sib).wait_send()
            for p in range(2):
                src, dst = part_send.at[t, tile, p], part_recv.at[t, tile, p]
                remote(src, dst, p_send.at[t, tile, p], p_recv.at[t, tile, p], sib).wait_send()
        for t in range(2):
            for p in range(2):
                part = hid.at[t + 1, tile, :, piece_cols(c, p)]
                remote(pan_send.at[t, tile, p], part, n_send.at[t, tile, p], n_recv.at[t, tile, p], up).wait_send()
                remote(part, part, r_send.at[t, tile, p], r_recv.at[t, tile, p], sib).wait_send()


def hand_over(panel, state, panel_out, state_out, panel_here, state_here, sem_in, sem_out):
    pieces = [(panel, panel_here, panel_out)]
    for i in range(4):
        rows = pl.ds(i * 1024, 1024)
        pieces.append((state.at[rows, :], state_here.at[rows, :], state_out.at[rows, :]))
    for i, (src, here, _) in enumerate(pieces):
        pltpu.make_async_copy(src, here, sem_in.at[i]).start()
    for i, (src, here, dst) in enumerate(pieces):
        pltpu.make_async_copy(src, here, sem_in.at[i]).wait()
        pltpu.make_async_copy(here, dst, sem_out.at[i]).start()
    for i, (_, here, dst) in enumerate(pieces):
        pltpu.make_async_copy(here, dst, sem_out.at[i]).wait()


def local(
    panels, feed, ssm_state, conv_state, w_in, w_out, norm_gain, conv_weight, conv_bias,
    dt_bias, decay_rate, skip_gain, out_gain,
):
    any_ = pl.BlockSpec(memory_space=pl.ANY)
    vmem = pl.BlockSpec(memory_space=pltpu.VMEM)
    dma = pltpu.SemaphoreType.DMA
    scratch = [
        pltpu.VMEM((9280, 128), BF16),
        pltpu.VMEM((STEPS, 128, 512), BF16),
        pltpu.VMEM((128, 640), BF16),
        pltpu.VMEM((8, 128), F32),
        pltpu.VMEM((STEPS, 2048, 512), BF16),
        pltpu.VMEM((2048, 640), BF16),
        pltpu.VMEM((HALF, WIDTH), BF16),
        pltpu.VMEM((3, 2, SEG, WIDTH), BF16),
        pltpu.VMEM((2 * SEG, WIDTH), BF16),
        pltpu.VMEM((2 * SEG, 128), F32),
        pltpu.VMEM((2 * SEG, 128), F32),
        pltpu.VMEM((2, 8, 5120), F32),
        pltpu.VMEM((2, STEPS, 8, CHUNK), F32),
        pltpu.VMEM((2, 8, 512), F32),
        pltpu.VMEM((2, 16, 512), BF16),
        pltpu.VMEM((2, 16, 512), BF16),
        pltpu.VMEM((2, HALF, 128), F32),
        pltpu.VMEM((2, STEPS, 128, CHUNK), F32),
        pltpu.VMEM((2, STEPS, 144, CHUNK), BF16),
        pltpu.VMEM((2, STEPS, 144, CHUNK), BF16),
        pltpu.VMEM((2, 2, SEG, 1024), BF16),
        pltpu.VMEM((4, SEG + 8, 128), F32),
        pltpu.VMEM((SEG, 640), F32),
        pltpu.VMEM((SEG, 512), F32),
        pltpu.VMEM((SEG, 512), F32),
        pltpu.VMEM((2, 2, SEG, 128), BF16),
        pltpu.VMEM((2, 2, SEG, 128), BF16),
        pltpu.VMEM((2, 2, SEG, 128), F32),
        pltpu.VMEM((2, 2, 32, 32), F32),
        pltpu.VMEM((2, SEG, 128), F32),
        pltpu.VMEM((2, 128, 256), F32),
        pltpu.VMEM((4 * SEG, 128), BF16),
        pltpu.VMEM((2, 8, 128), F32),
        pltpu.VMEM((2 * SEG, HALF), BF16),
        pltpu.VMEM((2, SEG, PIECE), F32),
        pltpu.VMEM((3, 2, 2, SEG, PIECE), BF16),
        pltpu.VMEM((3, 2, 2, SEG, PIECE), BF16),
        pltpu.VMEM((2 * SEG, 128), F32),
        pltpu.VMEM((3, 2, SEG, 128), F32),
        pltpu.VMEM((3, 2, SEG, 128), F32),
        pltpu.VMEM((2, 2, 2, SEG, PIECE), BF16),
        pltpu.VMEM((2, 2, SEG, PIECE), BF16),
        dma((9, 19)), dma((9, 19)), dma((7,)), dma((6,)), dma((6,)), dma((3, 2, 2)), dma((3, 2, 2)),
        dma((2, 2, 2)), dma((2, 2, 2)), dma((2, 2, 2)), dma((2, 2, 2)),
        dma((2, STEPS)), dma((2, STEPS)), dma((STEPS,)), dma((STEPS,)), dma((STEPS,)),
        dma((3, 2)), dma((3, 2)), dma((2,)), dma((2,)), dma((2,)),
    ]
    panel, state = pl.pallas_call(
        kernel,
        out_shape=(
            jax.ShapeDtypeStruct((SEG, WIDTH), BF16),
            jax.ShapeDtypeStruct((4096, 128), F32),
        ),
        in_specs=[any_] * 5 + [vmem] * 8,
        out_specs=(any_, any_),
        scratch_shapes=scratch,
        compiler_params=pltpu.CompilerParams(
            collective_id=0, has_side_effects=True, vmem_limit_bytes=60 * 1024 * 1024
        ),
        cost_estimate=pl.CostEstimate(flops=28_000_000_000, bytes_accessed=60_000_000, transcendentals=20_000_000),
    )(
        panels[0], feed, ssm_state.reshape(4096, 128), w_in[0].T, w_out[0], conv_state[0, 0],
        norm_gain, conv_weight[0], conv_bias, dt_bias, decay_rate, skip_gain, out_gain,
    )
    panel, state = pl.pallas_call(
        hand_over,
        out_shape=(jax.ShapeDtypeStruct((SEG, WIDTH), BF16), jax.ShapeDtypeStruct((4096, 128), F32)),
        in_specs=[any_, any_],
        out_specs=(any_, any_),
        scratch_shapes=[pltpu.VMEM((SEG, WIDTH), BF16), pltpu.VMEM((4096, 128), F32), dma((5,)), dma((5,))],
        compiler_params=pltpu.CompilerParams(vmem_limit_bytes=60 * 1024 * 1024),
    )(panel, state)
    return (panel[None], state.reshape(1, 1, 64, 64, 128))


def solution(mesh):
    return jax.shard_map(
        local,
        mesh=mesh,
        in_specs=(
            P("layer", "seq", None),
            P(None, "seq", None),
            P("layer", "seq", None, None, None),
            P("layer", "seq", None, None),
            P("layer", "seq", None),
            P("layer", None, None),
            P("layer", None),
            P("layer", None, None),
            P("layer", None),
            P("layer", None),
            P("layer", None),
            P("layer", None),
            P("layer", None),
        ),
        out_specs=(P("layer", "seq", None), P("layer", "seq", None, None, None)),
        check_vma=False,
    )
```

time: 237 us -> 221 us (0.932)
  Pallas kernels: 235 us -> 219 us
    pallas_call x1, Pallas kernels: 232 us -> 217 us  [local(): pl.pallas_call(kernel, out_shape=(jax.ShapeDtypeStruct((SEG, WIDTH), BF16...]
where the time goes in v3:
time: 221 us; the launch traced here: 220 us
  Pallas kernels  219 us (99%)
    pallas_call x1, Pallas kernels, local(): pl.pallas_call(kernel, out_shape=(jax.ShapeDtypeStruct((SEG, WIDTH), BF16...  217 us

profile of v3, /device:TPU:2, one launch (start us, length us, event | category | flops | bytes accessed | tf_op | source)
XLA Modules:
  0.0 220.3 jit_solution(11272451088662357328)
XLA Ops:
  0.6 216.8 %shard_map.140 = (bf16[160,2048]{1,0:T(8,128)(2,1)}, f32[4096,128]{1,0:T(8,128)}) custom-call(bf16[160,2048]{1,0:T(8,128)(2,1)} %bitcast.14, bf16[2,160,2048]{2,1,0:T(8,128)(2,1)} %feed.1, f32[4096,128]{1,0:T(8,128)} %bitcast.12, bf16[9280,128]{1,0:T(8,128)(2,1)} %bitcast.11, bf16[4096,2048]{1,0:T(8,128)(2,1)} %bitcast.10, bf16[3,5120]{1,0:T(4,128)(2,1)} %bitcast.17, ...), custom_call_target="tpu_custom_call" | custom-call | flops 28000000000 | bytes 60000000 | tf_op jit(solution)/shard_map/pallas_call | solution.py:692
  217.4 2.7 %shard_map.141 = (bf16[160,2048]{1,0:T(8,128)(2,1)}, f32[4096,128]{1,0:T(8,128)}) custom-call(bf16[160,2048]{1,0:T(8,128)(2,1)} %get-tuple-element.6.panel, f32[4096,128]{1,0:T(8,128)} %get-tuple-element.7.state), custom_call_target="tpu_custom_call" | custom-call | tf_op jit(solution)/shard_map/pallas_call | solution.py:709

commit v4 on v3

--- a/solution.py
+++ b/solution.py
@@ -125,6 +125,9 @@
             target[where, 256:512] = turned(8704 + cc * 256, 256)
             target[where, 512:640] = dt
         remote(bc_cut, w_bc.at[rows, :], g_send.at[8, 18], g_recv.at[8, 18], sib).start()
+        push(bc_part(m, c), 8, 2, to_z)
+        push(bc_part(m, c), 8, 0, to_yp)
+        push(bc_part(m, c), 8, 1, to_ym)
 
     def main_prepare(q):
         rows = pl.ds(own_rows, 128)
@@ -175,13 +178,20 @@
         push(part(m), q, 3, to_yp)
         push(part(m), q, 4, to_ym)
 
+    def landed_first(part, q, mm, slot):
+        if part is bc_part:
+            arrived(part(mm, c), q, slot)
+            arrived(part(mm, oc), q, slot + 3)
+        else:
+            arrived(part(mm), q, slot)
+
     def second_x(part, q):
-        arrived(part(o_y), q, 2)
+        landed_first(part, q, o_y, 2)
         push(part(o_y), q, 6, to_yp)
         push(part(o_y), q, 7, to_ym)
-        arrived(part(m_ym), q, 0)
+        landed_first(part, q, m_ym, 0)
         push(part(m_ym, 0), q, 8, to_yp)
-        arrived(part(m_yp), q, 1)
+        landed_first(part, q, m_yp, 1)
         push(part(m_yp, 1), q, 9, to_ym)
 
     def second_g(part, q):
@@ -218,7 +228,13 @@
         arrived(part(o_y2, 1), q, 17)
 
     def sent_x(part, q):
-        for slot in (0, 1, 2, 6, 7):
+        for slot in (0, 1, 2):
+            if part is bc_part:
+                sent(part(m, 0), q, slot)
+                sent(part(m, 0), q, slot + 3)
+            else:
+                sent(part(m), q, slot)
+        for slot in (6, 7):
             sent(part(m), q, slot)
         for slot in (8, 9, 14, 15):
             sent(part(m, 0), q, slot)
@@ -232,7 +248,9 @@
     bc_prepare()
     main_prepare(0)
     arrived(bc_landed(), 8, 18)
-    first_x(bc_part, 8)
+    push(bc_part(m, oc), 8, 5, to_z)
+    push(bc_part(m, oc), 8, 3, to_yp)
+    push(bc_part(m, oc), 8, 4, to_ym)
 
     @pl.loop(0, STEPS // 2)
     def _(i):
@@ -358,14 +376,16 @@
 
     low = lane < 64
 
-    def project(tile, q, into):
-        into[...] = dot(hg[tile * SEG : (tile + 1) * SEG, :], w_main[q])
+    def project(tile, q, into, half):
+        cols = slice(half * 256, half * 256 + 256)
+        into[:, cols] = dot(hg[tile * SEG : (tile + 1) * SEG, :], w_main[q, :, cols])
 
     def state_arrived(t, q):
         land = s_recv.at[t - 1, q]
         remote(land, land, st_send.at[t - 1, q], st_recv.at[t - 1, q], after).wait_recv()
 
-    def step_of(t, tile, q, made_of):
+    def step_of(t, tile, q, made_of, beside):
+        beside(0)
         rows = slice(tile * SEG, (tile + 1) * SEG)
         g = lax.div(q, 4)
         base = c * 32 + q * 4
@@ -390,6 +410,7 @@
         carried = dot(c_all[tile, g], state.astype(BF16))
         squares = jnp.zeros((SEG, 128), F32)
         grown = []
+        xs = []
         for pair in range(2):
             lanes = slice(pair * 128, pair * 128 + 128)
             cols = pl.ds(mult(c * HALF + q * CHUNK + pair * 128, 128), 128)
@@ -398,6 +419,12 @@
                 slot, x_tail(t, tile, q, pair, cols), made_of[:, lanes] * scale, 0.5 * conv_w[:, cols], 0.5 * conv_b[:, cols]
             )
             keep_tail(t, tile, slot, (x_loc, (min(t, 1), q, slice(0, 8), lanes)), (s_send, (min(t, 1), q, slice(128, 144), lanes)))
+            xs.append(x)
+        beside(1)
+        for pair in range(2):
+            lanes = slice(pair * 128, pair * 128 + 128)
+            cols = pl.ds(mult(c * HALF + q * CHUNK + pair * 128, 128), 128)
+            x = xs[pair]
             weights = []
             for h in (pair * 2, pair * 2 + 1):
                 col = jnp.broadcast_to(ld[:, h : h + 1], (SEG, 128))
@@ -448,20 +475,22 @@
     def piece_cols(half, p):
         return pl.ds(mult(half * 1024 + p * PIECE, PIECE), PIECE)
 
+    def panel_off(t, tile, p):
+        there = hid.at[t + 1, tile, :, piece_cols(c, p)]
+        remote(pan_send.at[t, tile, p], there, n_send.at[t, tile, p], n_recv.at[t, tile, p], up).start()
+
     def emit(t, tile):
         rows = slice(tile * SEG, (tile + 1) * SEG)
         sq_send[t, tile] = sq_mine[rows, :]
         remote(sq_send.at[t, tile], sq_recv.at[t, tile], q_send.at[t, tile], q_recv.at[t, tile], sib).start()
 
-        @pl.loop(0, 2)
-        def _(p):
+        for p in range(2):
             part_send[t, tile, p] = dot(gated[rows, :], w_o[:, piece_cols(oc, p)]).astype(BF16)
             remote(
                 part_send.at[t, tile, p], part_recv.at[t, tile, p], p_send.at[t, tile, p], p_recv.at[t, tile, p], sib
             ).start()
 
-        @pl.loop(0, 2)
-        def _(p):
+        for p in range(2):
             own_part[p] = dot(gated[rows, :], w_o[:, piece_cols(c, p)])
 
         if (t, tile) == (1, 0):
@@ -478,9 +507,8 @@
             if t < 2:
                 entering = fd[t, tile, :, p * PIECE : (p + 1) * PIECE].astype(F32)
                 pan_send[t, tile, p] = jnp.where(layer == 7, entering, panel).astype(BF16)
-                remote(
-                    pan_send.at[t, tile, p], hid.at[t + 1, tile, :, cols], n_send.at[t, tile, p], n_recv.at[t, tile, p], up
-                ).start()
+                if (t, tile) != (0, 1):
+                    panel_off(t, tile, p)
             else:
                 pan_stage[tile, p] = panel.astype(BF16)
 
@@ -530,7 +558,7 @@
     for tile in range(2):
         prologue(0, tile)
 
-    @pl.loop(0, STEPS)
+    @pl.loop(0, STEPS - 1)
     def _(q):
         @pl.when(lax.rem(q, 2) == 0)
         def _():
@@ -540,13 +568,18 @@
         def _():
             last_g(part_of(q), q)
 
-        project(0, q, made_a)
-        project(1, q, made_b)
-        step_of(0, 0, q, made_a)
-        step_of(0, 1, q, made_b)
+        for half in range(2):
+            project(0, q, made_a, half)
+        step_of(0, 0, q, made_a, functools.partial(project, 1, q, made_b))
+        step_of(0, 1, q, made_b, lambda half: None)
         state_off(0, 1, q)
 
+    last_g(part_of(STEPS - 1), STEPS - 1)
     for tile in range(2):
+        for half in range(2):
+            project(tile, STEPS - 1, made_a, half)
+        step_of(0, tile, STEPS - 1, made_a, lambda half: None)
+        state_off(0, tile, STEPS - 1)
         emit(0, tile)
 
     for t in (1, 2):
@@ -554,10 +587,14 @@
             ssq[tile * SEG : (tile + 1) * SEG, :] = jnp.zeros((SEG, 128), F32)
             if (t, tile) != (1, 1):
                 relay(t, tile)
+            if (t, tile) == (1, 0):
+                for p in range(2):
+                    panel_off(0, 1, p)
             receive(t, tile)
             prologue(t, tile)
 
-            project(tile, 0, made_a)
+            for half in range(2):
+                project(tile, 0, made_a, half)
 
             @pl.loop(0, STEPS // 2)
             def _(i):
@@ -565,10 +602,8 @@
                 if tile == 0:
                     state_arrived(t, q)
                     state_arrived(t, q + 1)
-                project(tile, q + 1, made_b)
-                step_of(t, tile, q, made_a)
-                project(tile, lax.rem(q + 2, STEPS), made_a)
-                step_of(t, tile, q + 1, made_b)
+                step_of(t, tile, q, made_a, functools.partial(project, tile, q + 1, made_b))
+                step_of(t, tile, q + 1, made_b, functools.partial(project, tile, lax.rem(q + 2, STEPS), made_a))
                 state_off(t, tile, q)
                 state_off(t, tile, q + 1)
 

time: 221 us -> 218 us (0.986)
  Pallas kernels: 219 us -> 216 us
    pallas_call x1, Pallas kernels: 217 us -> 213 us  [local(): pl.pallas_call(kernel, out_shape=(jax.ShapeDtypeStruct((SEG, WIDTH), BF16...]
where the time goes in v4:
time: 218 us; the launch traced here: 217 us
  Pallas kernels  216 us (99%)
    pallas_call x1, Pallas kernels, local(): pl.pallas_call(kernel, out_shape=(jax.ShapeDtypeStruct((SEG, WIDTH), BF16...  213 us

profile of v4, /device:TPU:2, one launch (start us, length us, event | category | flops | bytes accessed | tf_op | source)
XLA Modules:
  0.0 217.0 jit_solution(3370779945138959294)
XLA Ops:
  0.6 213.5 %shard_map.140 = (bf16[160,2048]{1,0:T(8,128)(2,1)}, f32[4096,128]{1,0:T(8,128)}) custom-call(bf16[160,2048]{1,0:T(8,128)(2,1)} %bitcast.14, bf16[2,160,2048]{2,1,0:T(8,128)(2,1)} %feed.1, f32[4096,128]{1,0:T(8,128)} %bitcast.12, bf16[9280,128]{1,0:T(8,128)(2,1)} %bitcast.11, bf16[4096,2048]{1,0:T(8,128)(2,1)} %bitcast.10, bf16[3,5120]{1,0:T(4,128)(2,1)} %bitcast.17, ...), custom_call_target="tpu_custom_call" | custom-call | flops 28000000000 | bytes 60000000 | tf_op jit(solution)/shard_map/pallas_call | solution.py:727
  214.1 2.7 %shard_map.141 = (bf16[160,2048]{1,0:T(8,128)(2,1)}, f32[4096,128]{1,0:T(8,128)}) custom-call(bf16[160,2048]{1,0:T(8,128)(2,1)} %get-tuple-element.6.panel, f32[4096,128]{1,0:T(8,128)} %get-tuple-element.7.state), custom_call_target="tpu_custom_call" | custom-call | tf_op jit(solution)/shard_map/pallas_call | solution.py:744

commit v5 on v4

--- a/solution.py
+++ b/solution.py
@@ -323,6 +323,10 @@
             target, at_ = away
             target[at_] = convbuf[slot, SEG - 8 : SEG + 8, :].astype(BF16)
 
+    def project(tile, q, into, half):
+        cols = slice(half * 256, half * 256 + 256)
+        into[:, cols] = dot(hg[tile * SEG : (tile + 1) * SEG, :], w_main[q, :, cols])
+
     def prologue(t, tile):
         rows = slice(tile * SEG, (tile + 1) * SEG)
         if t > 0 and tile == 0:
@@ -330,6 +334,9 @@
         total = jnp.sum(ssq[rows, :], axis=1, keepdims=True)
         rowscale[rows, :] = jnp.broadcast_to(lax.rsqrt(total * (1.0 / WIDTH) + EPS), (SEG, 128))
         proj[...] = dot(hg[rows, :], w_bc[...])
+        if t > 0:
+            for half in range(2):
+                project(tile, 0, made_a, half)
         causal = lane <= row
         tri = (
             lax.broadcasted_iota(jnp.int32, (SEG, SEG), 1) <= lax.broadcasted_iota(jnp.int32, (SEG, SEG), 0)
@@ -375,10 +382,6 @@
             remote(bc_to.at[t], bc_from.at[t], m_send.at[4 + t], m_recv.at[4 + t], after).start()
 
     low = lane < 64
-
-    def project(tile, q, into, half):
-        cols = slice(half * 256, half * 256 + 256)
-        into[:, cols] = dot(hg[tile * SEG : (tile + 1) * SEG, :], w_main[q, :, cols])
 
     def state_arrived(t, q):
         land = s_recv.at[t - 1, q]
@@ -490,8 +493,7 @@
                 part_send.at[t, tile, p], part_recv.at[t, tile, p], p_send.at[t, tile, p], p_recv.at[t, tile, p], sib
             ).start()
 
-        for p in range(2):
-            own_part[p] = dot(gated[rows, :], w_o[:, piece_cols(c, p)])
+        own_part[0] = dot(gated[rows, :], w_o[:, piece_cols(c, 0)])
 
         if (t, tile) == (1, 0):
             relay(1, 1)
@@ -501,6 +503,8 @@
         for p in range(2):
             land = part_recv.at[t, tile, p]
             remote(land, land, p_send.at[t, tile, p], p_recv.at[t, tile, p], sib).wait_recv()
+            if p == 1:
+                own_part[1] = dot(gated[rows, :], w_o[:, piece_cols(c, 1)])
             whole = own_part[p] + part_recv[t, tile, p].astype(F32)
             cols = piece_cols(c, p)
             panel = hid[t, tile, :, cols].astype(F32) + by_rows(whole, scale)
@@ -592,9 +596,6 @@
                     panel_off(0, 1, p)
             receive(t, tile)
             prologue(t, tile)
-
-            for half in range(2):
-                project(tile, 0, made_a, half)
 
             @pl.loop(0, STEPS // 2)
             def _(i):

time: 218 us -> 219 us (level)
  no operation moved by 1% of the time
where the time goes in v5:
time: 219 us; the launch traced here: 218 us
  Pallas kernels  217 us (99%)
    pallas_call x1, Pallas kernels, local(): pl.pallas_call(kernel, out_shape=(jax.ShapeDtypeStruct((SEG, WIDTH), BF16...  214 us

profile of v5, /device:TPU:2, one launch (start us, length us, event | category | flops | bytes accessed | tf_op | source)
XLA Modules:
  0.0 217.7 jit_solution(9177784330852662120)
XLA Ops:
  0.6 214.1 %shard_map.140 = (bf16[160,2048]{1,0:T(8,128)(2,1)}, f32[4096,128]{1,0:T(8,128)}) custom-call(bf16[160,2048]{1,0:T(8,128)(2,1)} %bitcast.14, bf16[2,160,2048]{2,1,0:T(8,128)(2,1)} %feed.1, f32[4096,128]{1,0:T(8,128)} %bitcast.12, bf16[9280,128]{1,0:T(8,128)(2,1)} %bitcast.11, bf16[4096,2048]{1,0:T(8,128)(2,1)} %bitcast.10, bf16[3,5120]{1,0:T(4,128)(2,1)} %bitcast.17, ...), custom_call_target="tpu_custom_call" | custom-call | flops 28000000000 | bytes 60000000 | tf_op jit(solution)/shard_map/pallas_call | solution.py:728
  214.8 2.7 %shard_map.141 = (bf16[160,2048]{1,0:T(8,128)(2,1)}, f32[4096,128]{1,0:T(8,128)}) custom-call(bf16[160,2048]{1,0:T(8,128)(2,1)} %get-tuple-element.6.panel, f32[4096,128]{1,0:T(8,128)} %get-tuple-element.7.state), custom_call_target="tpu_custom_call" | custom-call | tf_op jit(solution)/shard_map/pallas_call | solution.py:745
